TPU v7x, 768 devices: a whole 4x8x12 slice. The times are simulated.
768 devices in a mesh: depth: 12 (over z), row: 4 (over y_hi, core), col: 16 (over x, y_lo).
Axes of the slice: x: 4, y: 8 (y_hi: 2, y_lo: 4; y = y_hi * 4 + y_lo), z: 12, core: 2. Of those that a mesh axis runs over, the one named last changes fastest.
Arguments:
- phase: float32 [12, 256, 2048], P('depth', 'row', 'col'), may hold values from -1.8 to 1.8
- tilt: int32 [2, 2], replicated, may hold values from -6 to 6
- intensity: float32 [2, 256, 2048], P(None, 'row', 'col'), may hold values from 0.3 to 1.5
Outputs:
- grad_phase: float32 [12, 256, 2048], P('depth', 'row', 'col')
- exit_waves: float32 [2, 12, 2, 256, 2048], P(None, 'depth', None, 'row', 'col')
Inputs may be any that keep to these rules, and one draw needn't show every extreme that they name: `tilt`: whole numbers of phase cycles across the field.
All inputs are finite; a program needn't handle non-finite values.
Results may differ from a plain program's by a relative error of at most 0.0003.
Values sent between devices are 32-bit elements; how exact they have to be, the bound alone decides.
A program may use at most 32 MiB of HBM per device.

v0:
```python
import math

import jax
import jax.numpy as jnp
from jax import lax
from jax.sharding import PartitionSpec as P

HALO = 32
FRESNEL = 64


def extended_2(cells, sides, width):
    for axis, dim in sides:
        count = lax.axis_size(axis)
        ends = count - 1
        head = lax.slice_in_dim(cells, 0, width, axis=dim)
        tail = lax.slice_in_dim(cells, cells.shape[dim] - width, cells.shape[dim], axis=dim)
        cells = jnp.concatenate(
            [
                lax.ppermute(tail, axis, [(i, (i + 1) % count) for i in range(ends)]),
                cells,
                lax.ppermute(head, axis, [((i + 1) % count, i) for i in range(ends)]),
            ],
            axis=dim,
        )
    return cells


def from_behind(value, axis, steps):
    count = lax.axis_size(axis)
    leading, last = (max(0, -steps), min(count, count - steps))
    return lax.ppermute(value, axis, [(source, source + steps) for source in range(leading, last)])


def band_matrix(block_size, margin, fresnel, adjoint):
    shape_full = (block_size, block_size + 2 * margin)
    out_idx = lax.broadcasted_iota(jnp.int32, shape_full, 0)
    in_idx = lax.broadcasted_iota(jnp.int32, shape_full, 1)
    offset = (out_idx + margin - in_idx).astype(jnp.float32)
    inside = jnp.abs(offset) <= margin
    taper_dist = jnp.maximum(jnp.abs(offset) - 0.5 * margin, 0.0)
    profile = jnp.cos(jnp.pi * taper_dist / (margin + 2.0))
    weight = profile * profile / math.sqrt(fresnel)
    phase_angle = jnp.pi * offset * offset / fresnel
    real_part = jnp.where(inside, jnp.cos(phase_angle) * weight, 0.0)
    imag_part = jnp.where(inside, jnp.sin(phase_angle) * weight, 0.0)
    if adjoint:
        imag_part = -imag_part
    upper = jnp.stack([real_part, -imag_part])
    lower = jnp.stack([imag_part, real_part])
    return jnp.stack([upper, lower])


def along_rows(extended, matrix):
    pieces = [jnp.einsum("pqij,gqjc->gpic", matrix, extended, precision=lax.Precision.HIGHEST)]
    return jnp.concatenate(pieces, axis=2)


def along_cols(extended, matrix, margin):
    block_size = matrix.shape[2]
    extent = extended.shape[3] - 2 * margin
    pieces = []
    for block_start in range(0, extent, block_size):
        window = extended[:, :, :, block_start : block_start + block_size + 2 * margin]
        pieces.append(
            jnp.einsum("pqij,gqrj->gpri", matrix, window, precision=lax.Precision.HIGHEST)
        )
    return jnp.concatenate(pieces, axis=3)


def propagate(current, row_matrix, col_matrix):
    with_rows = extended_2(current, (("row", 2),), HALO)
    row_done = along_rows(with_rows, row_matrix)
    with_cols = extended_2(row_done, (("col", 3),), HALO)
    return along_cols(with_cols, col_matrix, HALO)


def transmit(screen, current, adjoint):
    screen_re = screen[0][None]
    screen_im = screen[1][None]
    if adjoint:
        screen_im = -screen_im
    real_part = screen_re * current[:, 0] - screen_im * current[:, 1]
    imag_part = screen_re * current[:, 1] + screen_im * current[:, 0]
    return jnp.stack([real_part, imag_part], axis=1)


def store_item(store, current, first_item, slice_index, active):
    begin = (first_item, jnp.int32(slice_index), jnp.int32(0), jnp.int32(0), jnp.int32(0))
    sizes_now = (current.shape[0], 1) + current.shape[1:]
    previous = lax.dynamic_slice(store, begin, sizes_now)
    fresh = jnp.where(active, current[:, None], previous)
    return lax.dynamic_update_slice(store, fresh, begin)


def body(phase, tilt, intensity):
    slices, tile_r, tile_c = phase.shape
    batch_size = tilt.shape[0]
    sections = lax.axis_size("depth")
    section_index = lax.axis_index("depth")
    group_size = 1
    groups = batch_size // group_size
    tick_count = sections + groups - 1
    block_r = 64
    block_c = 128
    fwd_rows = band_matrix(block_r, HALO, FRESNEL, False)
    fwd_cols = band_matrix(block_c, HALO, FRESNEL, False)
    adj_rows = band_matrix(block_r, HALO, FRESNEL, True)
    adj_cols = band_matrix(block_c, HALO, FRESNEL, True)
    row_pos = (
        lax.axis_index("row") * tile_r + lax.broadcasted_iota(jnp.int32, (tile_r, tile_c), 0)
    ).astype(jnp.float32)
    col_pos = (
        lax.axis_index("col") * tile_c + lax.broadcasted_iota(jnp.int32, (tile_r, tile_c), 1)
    ).astype(jnp.float32)
    height = float(tile_r * lax.axis_size("row"))
    width_all = float(tile_c * lax.axis_size("col"))
    tilt_f = tilt.astype(jnp.float32)
    phase_angle = (
        2.0
        * jnp.pi
        * (
            tilt_f[:, 0, None, None] * row_pos / height
            + tilt_f[:, 1, None, None] * col_pos / width_all
        )
    )
    incident = jnp.stack([jnp.cos(phase_angle), jnp.sin(phase_angle)], axis=1)
    screens = jnp.stack([jnp.cos(phase), jnp.sin(phase)], axis=1)

    def forward_tick(tick_now, carry):
        incoming, entering, leaving = carry
        group_index = tick_now - section_index
        active = (group_index >= 0) & (group_index < groups)
        first_item = jnp.clip(group_index, 0, groups - 1) * group_size
        current = jnp.where(
            section_index == 0,
            lax.dynamic_slice_in_dim(incident, first_item, group_size, 0),
            incoming,
        )
        entering = store_item(entering, current, first_item, 0, active)
        current = propagate(transmit(screens[0], current, False), fwd_rows, fwd_cols)
        leaving = store_item(leaving, current, first_item, 0, active)
        incoming = from_behind(current, "depth", 1)
        return (incoming, entering, leaving)

    store_zero = jnp.zeros((batch_size, slices, 2, tile_r, tile_c), jnp.float32)
    start_wave = jnp.zeros((group_size, 2, tile_r, tile_c), jnp.float32)
    _, entering, leaving = lax.fori_loop(
        0, tick_count, forward_tick, (start_wave, store_zero, store_zero)
    )
    final_wave = leaving[:, slices - 1]
    misfit = final_wave[:, 0] * final_wave[:, 0] + final_wave[:, 1] * final_wave[:, 1] - intensity
    seed_adjoint = 2.0 * misfit[:, None] * final_wave

    def backward_tick(tick_now, carry):
        incoming, gradient = carry
        group_index = tick_now - (sections - 1 - section_index)
        active = (group_index >= 0) & (group_index < groups)
        first_item = jnp.clip(group_index, 0, groups - 1) * group_size
        adjoint_wave = jnp.where(
            section_index == sections - 1,
            lax.dynamic_slice_in_dim(seed_adjoint, first_item, group_size, 0),
            incoming,
        )
        for slice_index in reversed(range(slices)):
            pulled = propagate(adjoint_wave, adj_rows, adj_cols)
            arrived = lax.dynamic_slice_in_dim(entering[:, slice_index], first_item, group_size, 0)
            moved = transmit(screens[slice_index], arrived, False)
            contribution = jnp.sum(pulled[:, 1] * moved[:, 0] - pulled[:, 0] * moved[:, 1], axis=0)
            gradient = gradient.at[slice_index].add(jnp.where(active, contribution, 0.0))
            adjoint_wave = transmit(screens[slice_index], pulled, True)
        incoming = from_behind(adjoint_wave, "depth", -1)
        return (incoming, gradient)

    grad_zero = jnp.zeros((slices, tile_r, tile_c), jnp.float32)
    _, gradient = lax.fori_loop(0, tick_count, backward_tick, (start_wave, grad_zero))
    return (gradient, leaving)


def solution(mesh):
    placed = (P("depth", "row", "col"), P(), P(None, "row", "col"))
    return jax.shard_map(
        body,
        mesh=mesh,
        in_specs=placed,
        out_specs=(P("depth", "row", "col"), P(None, "depth", None, "row", "col")),
        check_vma=False,
    )
```

profile of v0, /device:TPU:57, one launch (start us, length us, event | category | flops | bytes accessed | tf_op | source)
XLA Modules:
  0.0 780.9 jit_solution(2597610328308964907)
XLA Ops:
  4.1 382.7 %while.38 = (s32[]{:T(128)}, f32[1,2,64,128]{3,2,1,0:T(8,128)S(1)}, f32[2,1,2,64,128]{4,3,2,1,0:T(8,128)S(1)}, f32[2,1,2,64,128]{4,3,2,1,0:T(8,128)S(1)}, f32[1,...) while((s32[]{:T(128)}, f32[1,2,64,128]{3,2,1,0:T(8,128)S(1)}, ...), condition=%wide.region_1.2_spmd, body=%wide.region_0.1_spmd.sunk | while | flops 126091272 | bytes 2490761 | solution.py:148
  27.1 10.4 %collective-permute-start = (f32[1,2,32,128]{3,2,1,0:T(8,128)S(1)}, f32[1,2,32,128]{3,2,1,0:T(8,128)S(1)}, u32[]{:S(2)}, u32[]{:S(2)}) collective-permute-start(f32[1,2,32,128]{3,2,1,0:T(8,128)S(1)} %get-tuple-element.748), channel_id=1, source_target_pairs={{16,0},{32,16},{48,32},{17,1},{33,17},{49,33},{18,2},{34,18},{50,3... | collective-permute-start | bytes 98312 | tf_op jit(solution)/shard_map/while/body/eval_jaxpr/ppermute | solution.py:22
  42.9 6.7 collective-permute-start.3
  56.8 9.5 %collective-permute-start = (f32[1,2,32,128]{3,2,1,0:T(8,128)S(1)}, f32[1,2,32,128]{3,2,1,0:T(8,128)S(1)}, u32[]{:S(2)}, u32[]{:S(2)}) collective-permute-start(f32[1,2,32,128]{3,2,1,0:T(8,128)S(1)} %get-tuple-element.748), channel_id=1, source_target_pairs={{16,0},{32,16},{48,32},{17,1},{33,17},{49,33},{18,2},{34,18},{50,3... | collective-permute-start | bytes 98312 | tf_op jit(solution)/shard_map/while/body/eval_jaxpr/ppermute | solution.py:22
  71.8 6.7 collective-permute-start.3
  85.7 9.8 %collective-permute-start = (f32[1,2,32,128]{3,2,1,0:T(8,128)S(1)}, f32[1,2,32,128]{3,2,1,0:T(8,128)S(1)}, u32[]{:S(2)}, u32[]{:S(2)}) collective-permute-start(f32[1,2,32,128]{3,2,1,0:T(8,128)S(1)} %get-tuple-element.748), channel_id=1, source_target_pairs={{16,0},{32,16},{48,32},{17,1},{33,17},{49,33},{18,2},{34,18},{50,3... | collective-permute-start | bytes 98312 | tf_op jit(solution)/shard_map/while/body/eval_jaxpr/ppermute | solution.py:22
  100.9 6.7 collective-permute-start.3
  116.0 9.7 %collective-permute-start = (f32[1,2,32,128]{3,2,1,0:T(8,128)S(1)}, f32[1,2,32,128]{3,2,1,0:T(8,128)S(1)}, u32[]{:S(2)}, u32[]{:S(2)}) collective-permute-start(f32[1,2,32,128]{3,2,1,0:T(8,128)S(1)} %get-tuple-element.748), channel_id=1, source_target_pairs={{16,0},{32,16},{48,32},{17,1},{33,17},{49,33},{18,2},{34,18},{50,3... | collective-permute-start | bytes 98312 | tf_op jit(solution)/shard_map/while/body/eval_jaxpr/ppermute | solution.py:22
  131.1 6.7 collective-permute-start.3
  146.2 9.6 %collective-permute-start = (f32[1,2,32,128]{3,2,1,0:T(8,128)S(1)}, f32[1,2,32,128]{3,2,1,0:T(8,128)S(1)}, u32[]{:S(2)}, u32[]{:S(2)}) collective-permute-start(f32[1,2,32,128]{3,2,1,0:T(8,128)S(1)} %get-tuple-element.748), channel_id=1, source_target_pairs={{16,0},{32,16},{48,32},{17,1},{33,17},{49,33},{18,2},{34,18},{50,3... | collective-permute-start | bytes 98312 | tf_op jit(solution)/shard_map/while/body/eval_jaxpr/ppermute | solution.py:22
  161.2 6.7 collective-permute-start.3
  176.3 9.7 %collective-permute-start = (f32[1,2,32,128]{3,2,1,0:T(8,128)S(1)}, f32[1,2,32,128]{3,2,1,0:T(8,128)S(1)}, u32[]{:S(2)}, u32[]{:S(2)}) collective-permute-start(f32[1,2,32,128]{3,2,1,0:T(8,128)S(1)} %get-tuple-element.748), channel_id=1, source_target_pairs={{16,0},{32,16},{48,32},{17,1},{33,17},{49,33},{18,2},{34,18},{50,3... | collective-permute-start | bytes 98312 | tf_op jit(solution)/shard_map/while/body/eval_jaxpr/ppermute | solution.py:22
  191.3 6.7 collective-permute-start.3
  206.4 9.6 %collective-permute-start = (f32[1,2,32,128]{3,2,1,0:T(8,128)S(1)}, f32[1,2,32,128]{3,2,1,0:T(8,128)S(1)}, u32[]{:S(2)}, u32[]{:S(2)}) collective-permute-start(f32[1,2,32,128]{3,2,1,0:T(8,128)S(1)} %get-tuple-element.748), channel_id=1, source_target_pairs={{16,0},{32,16},{48,32},{17,1},{33,17},{49,33},{18,2},{34,18},{50,3... | collective-permute-start | bytes 98312 | tf_op jit(solution)/shard_map/while/body/eval_jaxpr/ppermute | solution.py:22
  221.4 6.7 collective-permute-start.3
  236.4 9.6 %collective-permute-start = (f32[1,2,32,128]{3,2,1,0:T(8,128)S(1)}, f32[1,2,32,128]{3,2,1,0:T(8,128)S(1)}, u32[]{:S(2)}, u32[]{:S(2)}) collective-permute-start(f32[1,2,32,128]{3,2,1,0:T(8,128)S(1)} %get-tuple-element.748), channel_id=1, source_target_pairs={{16,0},{32,16},{48,32},{17,1},{33,17},{49,33},{18,2},{34,18},{50,3... | collective-permute-start | bytes 98312 | tf_op jit(solution)/shard_map/while/body/eval_jaxpr/ppermute | solution.py:22
  251.5 6.7 collective-permute-start.3
  266.5 9.7 %collective-permute-start = (f32[1,2,32,128]{3,2,1,0:T(8,128)S(1)}, f32[1,2,32,128]{3,2,1,0:T(8,128)S(1)}, u32[]{:S(2)}, u32[]{:S(2)}) collective-permute-start(f32[1,2,32,128]{3,2,1,0:T(8,128)S(1)} %get-tuple-element.748), channel_id=1, source_target_pairs={{16,0},{32,16},{48,32},{17,1},{33,17},{49,33},{18,2},{34,18},{50,3... | collective-permute-start | bytes 98312 | tf_op jit(solution)/shard_map/while/body/eval_jaxpr/ppermute | solution.py:22
  281.6 6.7 collective-permute-start.3
  296.6 9.6 %collective-permute-start = (f32[1,2,32,128]{3,2,1,0:T(8,128)S(1)}, f32[1,2,32,128]{3,2,1,0:T(8,128)S(1)}, u32[]{:S(2)}, u32[]{:S(2)}) collective-permute-start(f32[1,2,32,128]{3,2,1,0:T(8,128)S(1)} %get-tuple-element.748), channel_id=1, source_target_pairs={{16,0},{32,16},{48,32},{17,1},{33,17},{49,33},{18,2},{34,18},{50,3... | collective-permute-start | bytes 98312 | tf_op jit(solution)/shard_map/while/body/eval_jaxpr/ppermute | solution.py:22
  311.6 6.7 collective-permute-start.3
  326.7 9.6 %collective-permute-start = (f32[1,2,32,128]{3,2,1,0:T(8,128)S(1)}, f32[1,2,32,128]{3,2,1,0:T(8,128)S(1)}, u32[]{:S(2)}, u32[]{:S(2)}) collective-permute-start(f32[1,2,32,128]{3,2,1,0:T(8,128)S(1)} %get-tuple-element.748), channel_id=1, source_target_pairs={{16,0},{32,16},{48,32},{17,1},{33,17},{49,33},{18,2},{34,18},{50,3... | collective-permute-start | bytes 98312 | tf_op jit(solution)/shard_map/while/body/eval_jaxpr/ppermute | solution.py:22
  356.8 9.7 %collective-permute-start = (f32[1,2,32,128]{3,2,1,0:T(8,128)S(1)}, f32[1,2,32,128]{3,2,1,0:T(8,128)S(1)}, u32[]{:S(2)}, u32[]{:S(2)}) collective-permute-start(f32[1,2,32,128]{3,2,1,0:T(8,128)S(1)} %get-tuple-element.748), channel_id=1, source_target_pairs={{16,0},{32,16},{48,32},{17,1},{33,17},{49,33},{18,2},{34,18},{50,3... | collective-permute-start | bytes 98312 | tf_op jit(solution)/shard_map/while/body/eval_jaxpr/ppermute | solution.py:22
  371.8 6.7 collective-permute-start.3
  387.6 392.6 %while.39 = (s32[]{:T(128)}, f32[1,2,64,128]{3,2,1,0:T(8,128)S(1)}, f32[1,64,128]{2,1,0:T(8,128)S(1)}, f32[1,2,64,128]{3,2,1,0:T(8,128)S(1)}, pred[]{:T(512)}, /...) while((s32[]{:T(128)}, f32[1,2,64,128]{3,2,1,0:T(8,128)S(1)}, ...), condition=%wide.region_3.4_spmd.clone, body=%wide.region_2.3_spmd.clone.sunk | while | flops 126124032 | bytes 2654618 | solution.py:176
  387.7 9.6 %collective-permute-start.5 = (f32[1,2,32,128]{3,2,1,0:T(8,128)S(1)}, f32[1,2,32,128]{3,2,1,0:T(8,128)S(1)}, u32[]{:S(2)}, u32[]{:S(2)}) collective-permute-start(f32[1,2,32,128]{3,2,1,0:T(8,128)S(1)} %get-tuple-element.766), channel_id=1, source_target_pairs={{16,0},{32,16},{48,32},{17,1},{33,17},{49,33},{18,2},{34,18},{50,3... | collective-permute-start | bytes 98312 | tf_op jit(solution)/shard_map/while/body/eval_jaxpr/ppermute | solution.py:22
  418.1 9.7 %collective-permute-start.5 = (f32[1,2,32,128]{3,2,1,0:T(8,128)S(1)}, f32[1,2,32,128]{3,2,1,0:T(8,128)S(1)}, u32[]{:S(2)}, u32[]{:S(2)}) collective-permute-start(f32[1,2,32,128]{3,2,1,0:T(8,128)S(1)} %get-tuple-element.766), channel_id=1, source_target_pairs={{16,0},{32,16},{48,32},{17,1},{33,17},{49,33},{18,2},{34,18},{50,3... | collective-permute-start | bytes 98312 | tf_op jit(solution)/shard_map/while/body/eval_jaxpr/ppermute | solution.py:22
  448.5 9.6 %collective-permute-start.5 = (f32[1,2,32,128]{3,2,1,0:T(8,128)S(1)}, f32[1,2,32,128]{3,2,1,0:T(8,128)S(1)}, u32[]{:S(2)}, u32[]{:S(2)}) collective-permute-start(f32[1,2,32,128]{3,2,1,0:T(8,128)S(1)} %get-tuple-element.766), channel_id=1, source_target_pairs={{16,0},{32,16},{48,32},{17,1},{33,17},{49,33},{18,2},{34,18},{50,3... | collective-permute-start | bytes 98312 | tf_op jit(solution)/shard_map/while/body/eval_jaxpr/ppermute | solution.py:22
  463.6 6.7 collective-permute-start.8
  479.0 9.7 %collective-permute-start.5 = (f32[1,2,32,128]{3,2,1,0:T(8,128)S(1)}, f32[1,2,32,128]{3,2,1,0:T(8,128)S(1)}, u32[]{:S(2)}, u32[]{:S(2)}) collective-permute-start(f32[1,2,32,128]{3,2,1,0:T(8,128)S(1)} %get-tuple-element.766), channel_id=1, source_target_pairs={{16,0},{32,16},{48,32},{17,1},{33,17},{49,33},{18,2},{34,18},{50,3... | collective-permute-start | bytes 98312 | tf_op jit(solution)/shard_map/while/body/eval_jaxpr/ppermute | solution.py:22
  509.4 9.6 %collective-permute-start.5 = (f32[1,2,32,128]{3,2,1,0:T(8,128)S(1)}, f32[1,2,32,128]{3,2,1,0:T(8,128)S(1)}, u32[]{:S(2)}, u32[]{:S(2)}) collective-permute-start(f32[1,2,32,128]{3,2,1,0:T(8,128)S(1)} %get-tuple-element.766), channel_id=1, source_target_pairs={{16,0},{32,16},{48,32},{17,1},{33,17},{49,33},{18,2},{34,18},{50,3... | collective-permute-start | bytes 98312 | tf_op jit(solution)/shard_map/while/body/eval_jaxpr/ppermute | solution.py:22
  524.4 6.7 collective-permute-start.8
  539.6 9.7 %collective-permute-start.5 = (f32[1,2,32,128]{3,2,1,0:T(8,128)S(1)}, f32[1,2,32,128]{3,2,1,0:T(8,128)S(1)}, u32[]{:S(2)}, u32[]{:S(2)}) collective-permute-start(f32[1,2,32,128]{3,2,1,0:T(8,128)S(1)} %get-tuple-element.766), channel_id=1, source_target_pairs={{16,0},{32,16},{48,32},{17,1},{33,17},{49,33},{18,2},{34,18},{50,3... | collective-permute-start | bytes 98312 | tf_op jit(solution)/shard_map/while/body/eval_jaxpr/ppermute | solution.py:22
  554.6 6.7 collective-permute-start.8
  569.7 9.7 %collective-permute-start.5 = (f32[1,2,32,128]{3,2,1,0:T(8,128)S(1)}, f32[1,2,32,128]{3,2,1,0:T(8,128)S(1)}, u32[]{:S(2)}, u32[]{:S(2)}) collective-permute-start(f32[1,2,32,128]{3,2,1,0:T(8,128)S(1)} %get-tuple-element.766), channel_id=1, source_target_pairs={{16,0},{32,16},{48,32},{17,1},{33,17},{49,33},{18,2},{34,18},{50,3... | collective-permute-start | bytes 98312 | tf_op jit(solution)/shard_map/while/body/eval_jaxpr/ppermute | solution.py:22
  584.7 6.7 collective-permute-start.8
  599.7 9.7 %collective-permute-start.5 = (f32[1,2,32,128]{3,2,1,0:T(8,128)S(1)}, f32[1,2,32,128]{3,2,1,0:T(8,128)S(1)}, u32[]{:S(2)}, u32[]{:S(2)}) collective-permute-start(f32[1,2,32,128]{3,2,1,0:T(8,128)S(1)} %get-tuple-element.766), channel_id=1, source_target_pairs={{16,0},{32,16},{48,32},{17,1},{33,17},{49,33},{18,2},{34,18},{50,3... | collective-permute-start | bytes 98312 | tf_op jit(solution)/shard_map/while/body/eval_jaxpr/ppermute | solution.py:22
  614.8 6.7 collective-permute-start.8
  629.8 9.7 %collective-permute-start.5 = (f32[1,2,32,128]{3,2,1,0:T(8,128)S(1)}, f32[1,2,32,128]{3,2,1,0:T(8,128)S(1)}, u32[]{:S(2)}, u32[]{:S(2)}) collective-permute-start(f32[1,2,32,128]{3,2,1,0:T(8,128)S(1)} %get-tuple-element.766), channel_id=1, source_target_pairs={{16,0},{32,16},{48,32},{17,1},{33,17},{49,33},{18,2},{34,18},{50,3... | collective-permute-start | bytes 98312 | tf_op jit(solution)/shard_map/while/body/eval_jaxpr/ppermute | solution.py:22
  644.9 6.7 collective-permute-start.8
  659.9 9.7 %collective-permute-start.5 = (f32[1,2,32,128]{3,2,1,0:T(8,128)S(1)}, f32[1,2,32,128]{3,2,1,0:T(8,128)S(1)}, u32[]{:S(2)}, u32[]{:S(2)}) collective-permute-start(f32[1,2,32,128]{3,2,1,0:T(8,128)S(1)} %get-tuple-element.766), channel_id=1, source_target_pairs={{16,0},{32,16},{48,32},{17,1},{33,17},{49,33},{18,2},{34,18},{50,3... | collective-permute-start | bytes 98312 | tf_op jit(solution)/shard_map/while/body/eval_jaxpr/ppermute | solution.py:22
  675.0 6.7 collective-permute-start.8
  690.0 9.7 %collective-permute-start.5 = (f32[1,2,32,128]{3,2,1,0:T(8,128)S(1)}, f32[1,2,32,128]{3,2,1,0:T(8,128)S(1)}, u32[]{:S(2)}, u32[]{:S(2)}) collective-permute-start(f32[1,2,32,128]{3,2,1,0:T(8,128)S(1)} %get-tuple-element.766), channel_id=1, source_target_pairs={{16,0},{32,16},{48,32},{17,1},{33,17},{49,33},{18,2},{34,18},{50,3... | collective-permute-start | bytes 98312 | tf_op jit(solution)/shard_map/while/body/eval_jaxpr/ppermute | solution.py:22
  705.1 6.7 collective-permute-start.8
  720.1 9.7 %collective-permute-start.5 = (f32[1,2,32,128]{3,2,1,0:T(8,128)S(1)}, f32[1,2,32,128]{3,2,1,0:T(8,128)S(1)}, u32[]{:S(2)}, u32[]{:S(2)}) collective-permute-start(f32[1,2,32,128]{3,2,1,0:T(8,128)S(1)} %get-tuple-element.766), channel_id=1, source_target_pairs={{16,0},{32,16},{48,32},{17,1},{33,17},{49,33},{18,2},{34,18},{50,3... | collective-permute-start | bytes 98312 | tf_op jit(solution)/shard_map/while/body/eval_jaxpr/ppermute | solution.py:22
  735.2 6.7 collective-permute-start.8
  750.2 9.7 %collective-permute-start.5 = (f32[1,2,32,128]{3,2,1,0:T(8,128)S(1)}, f32[1,2,32,128]{3,2,1,0:T(8,128)S(1)}, u32[]{:S(2)}, u32[]{:S(2)}) collective-permute-start(f32[1,2,32,128]{3,2,1,0:T(8,128)S(1)} %get-tuple-element.766), channel_id=1, source_target_pairs={{16,0},{32,16},{48,32},{17,1},{33,17},{49,33},{18,2},{34,18},{50,3... | collective-permute-start | bytes 98312 | tf_op jit(solution)/shard_map/while/body/eval_jaxpr/ppermute | solution.py:22
  765.2 6.7 collective-permute-start.8
  (443 shorter events, 394.5 us)
Async XLA Ops:
  27.1 11.7 %collective-permute-start = (f32[1,2,32,128]{3,2,1,0:T(8,128)S(1)}, f32[1,2,32,128]{3,2,1,0:T(8,128)S(1)}, u32[]{:S(2)}, u32[]{:S(2)}) collective-permute-start(f32[1,2,32,128]{3,2,1,0:T(8,128)S(1)} %get-tuple-element.748), channel_id=1, source_target_pairs={{16,0},{32,16},{48,32},{17,1},{33,17},{49,33},{18,2},{34,18},{50,3... | collective-permute-start | bytes 98312 | tf_op jit(solution)/shard_map/while/body/eval_jaxpr/ppermute | solution.py:22
  41.0 8.6 %collective-permute-start.2 = (f32[1,2,64,32]{3,2,1,0:T(8,128)S(1)}, f32[1,2,64,32]{3,2,1,0:T(8,128)S(1)}, u32[]{:S(2)}, u32[]{:S(2)}) collective-permute-start(f32[1,2,64,32]{3,2,1,0:T(8,128)S(1)} %get-tuple-element.750), channel_id=1, source_target_pairs={{1,0},{2,1},{3,2},{4,3},{5,4},{6,5},{7,6},{8,7},{9,8},{10,9},{11,1... | collective-permute-start | bytes 49160 | tf_op jit(solution)/shard_map/while/body/eval_jaxpr/ppermute | solution.py:22
  56.8 10.9 %collective-permute-start = (f32[1,2,32,128]{3,2,1,0:T(8,128)S(1)}, f32[1,2,32,128]{3,2,1,0:T(8,128)S(1)}, u32[]{:S(2)}, u32[]{:S(2)}) collective-permute-start(f32[1,2,32,128]{3,2,1,0:T(8,128)S(1)} %get-tuple-element.748), channel_id=1, source_target_pairs={{16,0},{32,16},{48,32},{17,1},{33,17},{49,33},{18,2},{34,18},{50,3... | collective-permute-start | bytes 98312 | tf_op jit(solution)/shard_map/while/body/eval_jaxpr/ppermute | solution.py:22
  69.8 8.6 %collective-permute-start.2 = (f32[1,2,64,32]{3,2,1,0:T(8,128)S(1)}, f32[1,2,64,32]{3,2,1,0:T(8,128)S(1)}, u32[]{:S(2)}, u32[]{:S(2)}) collective-permute-start(f32[1,2,64,32]{3,2,1,0:T(8,128)S(1)} %get-tuple-element.750), channel_id=1, source_target_pairs={{1,0},{2,1},{3,2},{4,3},{5,4},{6,5},{7,6},{8,7},{9,8},{10,9},{11,1... | collective-permute-start | bytes 49160 | tf_op jit(solution)/shard_map/while/body/eval_jaxpr/ppermute | solution.py:22
  85.7 11.1 %collective-permute-start = (f32[1,2,32,128]{3,2,1,0:T(8,128)S(1)}, f32[1,2,32,128]{3,2,1,0:T(8,128)S(1)}, u32[]{:S(2)}, u32[]{:S(2)}) collective-permute-start(f32[1,2,32,128]{3,2,1,0:T(8,128)S(1)} %get-tuple-element.748), channel_id=1, source_target_pairs={{16,0},{32,16},{48,32},{17,1},{33,17},{49,33},{18,2},{34,18},{50,3... | collective-permute-start | bytes 98312 | tf_op jit(solution)/shard_map/while/body/eval_jaxpr/ppermute | solution.py:22
  98.9 8.6 %collective-permute-start.2 = (f32[1,2,64,32]{3,2,1,0:T(8,128)S(1)}, f32[1,2,64,32]{3,2,1,0:T(8,128)S(1)}, u32[]{:S(2)}, u32[]{:S(2)}) collective-permute-start(f32[1,2,64,32]{3,2,1,0:T(8,128)S(1)} %get-tuple-element.750), channel_id=1, source_target_pairs={{1,0},{2,1},{3,2},{4,3},{5,4},{6,5},{7,6},{8,7},{9,8},{10,9},{11,1... | collective-permute-start | bytes 49160 | tf_op jit(solution)/shard_map/while/body/eval_jaxpr/ppermute | solution.py:22
  116.0 11.0 %collective-permute-start = (f32[1,2,32,128]{3,2,1,0:T(8,128)S(1)}, f32[1,2,32,128]{3,2,1,0:T(8,128)S(1)}, u32[]{:S(2)}, u32[]{:S(2)}) collective-permute-start(f32[1,2,32,128]{3,2,1,0:T(8,128)S(1)} %get-tuple-element.748), channel_id=1, source_target_pairs={{16,0},{32,16},{48,32},{17,1},{33,17},{49,33},{18,2},{34,18},{50,3... | collective-permute-start | bytes 98312 | tf_op jit(solution)/shard_map/while/body/eval_jaxpr/ppermute | solution.py:22
  129.1 8.6 %collective-permute-start.2 = (f32[1,2,64,32]{3,2,1,0:T(8,128)S(1)}, f32[1,2,64,32]{3,2,1,0:T(8,128)S(1)}, u32[]{:S(2)}, u32[]{:S(2)}) collective-permute-start(f32[1,2,64,32]{3,2,1,0:T(8,128)S(1)} %get-tuple-element.750), channel_id=1, source_target_pairs={{1,0},{2,1},{3,2},{4,3},{5,4},{6,5},{7,6},{8,7},{9,8},{10,9},{11,1... | collective-permute-start | bytes 49160 | tf_op jit(solution)/shard_map/while/body/eval_jaxpr/ppermute | solution.py:22
  146.2 11.0 %collective-permute-start = (f32[1,2,32,128]{3,2,1,0:T(8,128)S(1)}, f32[1,2,32,128]{3,2,1,0:T(8,128)S(1)}, u32[]{:S(2)}, u32[]{:S(2)}) collective-permute-start(f32[1,2,32,128]{3,2,1,0:T(8,128)S(1)} %get-tuple-element.748), channel_id=1, source_target_pairs={{16,0},{32,16},{48,32},{17,1},{33,17},{49,33},{18,2},{34,18},{50,3... | collective-permute-start | bytes 98312 | tf_op jit(solution)/shard_map/while/body/eval_jaxpr/ppermute | solution.py:22
  159.3 8.6 %collective-permute-start.2 = (f32[1,2,64,32]{3,2,1,0:T(8,128)S(1)}, f32[1,2,64,32]{3,2,1,0:T(8,128)S(1)}, u32[]{:S(2)}, u32[]{:S(2)}) collective-permute-start(f32[1,2,64,32]{3,2,1,0:T(8,128)S(1)} %get-tuple-element.750), channel_id=1, source_target_pairs={{1,0},{2,1},{3,2},{4,3},{5,4},{6,5},{7,6},{8,7},{9,8},{10,9},{11,1... | collective-permute-start | bytes 49160 | tf_op jit(solution)/shard_map/while/body/eval_jaxpr/ppermute | solution.py:22
  176.3 11.0 %collective-permute-start = (f32[1,2,32,128]{3,2,1,0:T(8,128)S(1)}, f32[1,2,32,128]{3,2,1,0:T(8,128)S(1)}, u32[]{:S(2)}, u32[]{:S(2)}) collective-permute-start(f32[1,2,32,128]{3,2,1,0:T(8,128)S(1)} %get-tuple-element.748), channel_id=1, source_target_pairs={{16,0},{32,16},{48,32},{17,1},{33,17},{49,33},{18,2},{34,18},{50,3... | collective-permute-start | bytes 98312 | tf_op jit(solution)/shard_map/while/body/eval_jaxpr/ppermute | solution.py:22
  189.4 8.6 %collective-permute-start.2 = (f32[1,2,64,32]{3,2,1,0:T(8,128)S(1)}, f32[1,2,64,32]{3,2,1,0:T(8,128)S(1)}, u32[]{:S(2)}, u32[]{:S(2)}) collective-permute-start(f32[1,2,64,32]{3,2,1,0:T(8,128)S(1)} %get-tuple-element.750), channel_id=1, source_target_pairs={{1,0},{2,1},{3,2},{4,3},{5,4},{6,5},{7,6},{8,7},{9,8},{10,9},{11,1... | collective-permute-start | bytes 49160 | tf_op jit(solution)/shard_map/while/body/eval_jaxpr/ppermute | solution.py:22
  206.4 11.0 %collective-permute-start = (f32[1,2,32,128]{3,2,1,0:T(8,128)S(1)}, f32[1,2,32,128]{3,2,1,0:T(8,128)S(1)}, u32[]{:S(2)}, u32[]{:S(2)}) collective-permute-start(f32[1,2,32,128]{3,2,1,0:T(8,128)S(1)} %get-tuple-element.748), channel_id=1, source_target_pairs={{16,0},{32,16},{48,32},{17,1},{33,17},{49,33},{18,2},{34,18},{50,3... | collective-permute-start | bytes 98312 | tf_op jit(solution)/shard_map/while/body/eval_jaxpr/ppermute | solution.py:22
  219.5 8.6 %collective-permute-start.2 = (f32[1,2,64,32]{3,2,1,0:T(8,128)S(1)}, f32[1,2,64,32]{3,2,1,0:T(8,128)S(1)}, u32[]{:S(2)}, u32[]{:S(2)}) collective-permute-start(f32[1,2,64,32]{3,2,1,0:T(8,128)S(1)} %get-tuple-element.750), channel_id=1, source_target_pairs={{1,0},{2,1},{3,2},{4,3},{5,4},{6,5},{7,6},{8,7},{9,8},{10,9},{11,1... | collective-permute-start | bytes 49160 | tf_op jit(solution)/shard_map/while/body/eval_jaxpr/ppermute | solution.py:22
  236.4 11.0 %collective-permute-start = (f32[1,2,32,128]{3,2,1,0:T(8,128)S(1)}, f32[1,2,32,128]{3,2,1,0:T(8,128)S(1)}, u32[]{:S(2)}, u32[]{:S(2)}) collective-permute-start(f32[1,2,32,128]{3,2,1,0:T(8,128)S(1)} %get-tuple-element.748), channel_id=1, source_target_pairs={{16,0},{32,16},{48,32},{17,1},{33,17},{49,33},{18,2},{34,18},{50,3... | collective-permute-start | bytes 98312 | tf_op jit(solution)/shard_map/while/body/eval_jaxpr/ppermute | solution.py:22
  249.6 8.6 %collective-permute-start.2 = (f32[1,2,64,32]{3,2,1,0:T(8,128)S(1)}, f32[1,2,64,32]{3,2,1,0:T(8,128)S(1)}, u32[]{:S(2)}, u32[]{:S(2)}) collective-permute-start(f32[1,2,64,32]{3,2,1,0:T(8,128)S(1)} %get-tuple-element.750), channel_id=1, source_target_pairs={{1,0},{2,1},{3,2},{4,3},{5,4},{6,5},{7,6},{8,7},{9,8},{10,9},{11,1... | collective-permute-start | bytes 49160 | tf_op jit(solution)/shard_map/while/body/eval_jaxpr/ppermute | solution.py:22
  266.5 11.0 %collective-permute-start = (f32[1,2,32,128]{3,2,1,0:T(8,128)S(1)}, f32[1,2,32,128]{3,2,1,0:T(8,128)S(1)}, u32[]{:S(2)}, u32[]{:S(2)}) collective-permute-start(f32[1,2,32,128]{3,2,1,0:T(8,128)S(1)} %get-tuple-element.748), channel_id=1, source_target_pairs={{16,0},{32,16},{48,32},{17,1},{33,17},{49,33},{18,2},{34,18},{50,3... | collective-permute-start | bytes 98312 | tf_op jit(solution)/shard_map/while/body/eval_jaxpr/ppermute | solution.py:22
  279.6 8.6 %collective-permute-start.2 = (f32[1,2,64,32]{3,2,1,0:T(8,128)S(1)}, f32[1,2,64,32]{3,2,1,0:T(8,128)S(1)}, u32[]{:S(2)}, u32[]{:S(2)}) collective-permute-start(f32[1,2,64,32]{3,2,1,0:T(8,128)S(1)} %get-tuple-element.750), channel_id=1, source_target_pairs={{1,0},{2,1},{3,2},{4,3},{5,4},{6,5},{7,6},{8,7},{9,8},{10,9},{11,1... | collective-permute-start | bytes 49160 | tf_op jit(solution)/shard_map/while/body/eval_jaxpr/ppermute | solution.py:22
  296.6 11.0 %collective-permute-start = (f32[1,2,32,128]{3,2,1,0:T(8,128)S(1)}, f32[1,2,32,128]{3,2,1,0:T(8,128)S(1)}, u32[]{:S(2)}, u32[]{:S(2)}) collective-permute-start(f32[1,2,32,128]{3,2,1,0:T(8,128)S(1)} %get-tuple-element.748), channel_id=1, source_target_pairs={{16,0},{32,16},{48,32},{17,1},{33,17},{49,33},{18,2},{34,18},{50,3... | collective-permute-start | bytes 98312 | tf_op jit(solution)/shard_map/while/body/eval_jaxpr/ppermute | solution.py:22
  326.7 11.0 %collective-permute-start = (f32[1,2,32,128]{3,2,1,0:T(8,128)S(1)}, f32[1,2,32,128]{3,2,1,0:T(8,128)S(1)}, u32[]{:S(2)}, u32[]{:S(2)}) collective-permute-start(f32[1,2,32,128]{3,2,1,0:T(8,128)S(1)} %get-tuple-element.748), channel_id=1, source_target_pairs={{16,0},{32,16},{48,32},{17,1},{33,17},{49,33},{18,2},{34,18},{50,3... | collective-permute-start | bytes 98312 | tf_op jit(solution)/shard_map/while/body/eval_jaxpr/ppermute | solution.py:22
  356.8 11.0 %collective-permute-start = (f32[1,2,32,128]{3,2,1,0:T(8,128)S(1)}, f32[1,2,32,128]{3,2,1,0:T(8,128)S(1)}, u32[]{:S(2)}, u32[]{:S(2)}) collective-permute-start(f32[1,2,32,128]{3,2,1,0:T(8,128)S(1)} %get-tuple-element.748), channel_id=1, source_target_pairs={{16,0},{32,16},{48,32},{17,1},{33,17},{49,33},{18,2},{34,18},{50,3... | collective-permute-start | bytes 98312 | tf_op jit(solution)/shard_map/while/body/eval_jaxpr/ppermute | solution.py:22
  369.9 8.6 %collective-permute-start.2 = (f32[1,2,64,32]{3,2,1,0:T(8,128)S(1)}, f32[1,2,64,32]{3,2,1,0:T(8,128)S(1)}, u32[]{:S(2)}, u32[]{:S(2)}) collective-permute-start(f32[1,2,64,32]{3,2,1,0:T(8,128)S(1)} %get-tuple-element.750), channel_id=1, source_target_pairs={{1,0},{2,1},{3,2},{4,3},{5,4},{6,5},{7,6},{8,7},{9,8},{10,9},{11,1... | collective-permute-start | bytes 49160 | tf_op jit(solution)/shard_map/while/body/eval_jaxpr/ppermute | solution.py:22
  387.7 11.0 %collective-permute-start.5 = (f32[1,2,32,128]{3,2,1,0:T(8,128)S(1)}, f32[1,2,32,128]{3,2,1,0:T(8,128)S(1)}, u32[]{:S(2)}, u32[]{:S(2)}) collective-permute-start(f32[1,2,32,128]{3,2,1,0:T(8,128)S(1)} %get-tuple-element.766), channel_id=1, source_target_pairs={{16,0},{32,16},{48,32},{17,1},{33,17},{49,33},{18,2},{34,18},{50,3... | collective-permute-start | bytes 98312 | tf_op jit(solution)/shard_map/while/body/eval_jaxpr/ppermute | solution.py:22
  400.8 8.7 %collective-permute-start.7 = (f32[1,2,64,32]{3,2,1,0:T(8,128)S(1)}, f32[1,2,64,32]{3,2,1,0:T(8,128)S(1)}, u32[]{:S(2)}, u32[]{:S(2)}) collective-permute-start(f32[1,2,64,32]{3,2,1,0:T(8,128)S(1)} %get-tuple-element.768), channel_id=1, source_target_pairs={{1,0},{2,1},{3,2},{4,3},{5,4},{6,5},{7,6},{8,7},{9,8},{10,9},{11,1... | collective-permute-start | bytes 49160 | tf_op jit(solution)/shard_map/while/body/eval_jaxpr/ppermute | solution.py:22
  418.1 11.0 %collective-permute-start.5 = (f32[1,2,32,128]{3,2,1,0:T(8,128)S(1)}, f32[1,2,32,128]{3,2,1,0:T(8,128)S(1)}, u32[]{:S(2)}, u32[]{:S(2)}) collective-permute-start(f32[1,2,32,128]{3,2,1,0:T(8,128)S(1)} %get-tuple-element.766), channel_id=1, source_target_pairs={{16,0},{32,16},{48,32},{17,1},{33,17},{49,33},{18,2},{34,18},{50,3... | collective-permute-start | bytes 98312 | tf_op jit(solution)/shard_map/while/body/eval_jaxpr/ppermute | solution.py:22
  431.2 8.7 %collective-permute-start.7 = (f32[1,2,64,32]{3,2,1,0:T(8,128)S(1)}, f32[1,2,64,32]{3,2,1,0:T(8,128)S(1)}, u32[]{:S(2)}, u32[]{:S(2)}) collective-permute-start(f32[1,2,64,32]{3,2,1,0:T(8,128)S(1)} %get-tuple-element.768), channel_id=1, source_target_pairs={{1,0},{2,1},{3,2},{4,3},{5,4},{6,5},{7,6},{8,7},{9,8},{10,9},{11,1... | collective-permute-start | bytes 49160 | tf_op jit(solution)/shard_map/while/body/eval_jaxpr/ppermute | solution.py:22
  448.5 11.0 %collective-permute-start.5 = (f32[1,2,32,128]{3,2,1,0:T(8,128)S(1)}, f32[1,2,32,128]{3,2,1,0:T(8,128)S(1)}, u32[]{:S(2)}, u32[]{:S(2)}) collective-permute-start(f32[1,2,32,128]{3,2,1,0:T(8,128)S(1)} %get-tuple-element.766), channel_id=1, source_target_pairs={{16,0},{32,16},{48,32},{17,1},{33,17},{49,33},{18,2},{34,18},{50,3... | collective-permute-start | bytes 98312 | tf_op jit(solution)/shard_map/while/body/eval_jaxpr/ppermute | solution.py:22
  461.6 8.7 %collective-permute-start.7 = (f32[1,2,64,32]{3,2,1,0:T(8,128)S(1)}, f32[1,2,64,32]{3,2,1,0:T(8,128)S(1)}, u32[]{:S(2)}, u32[]{:S(2)}) collective-permute-start(f32[1,2,64,32]{3,2,1,0:T(8,128)S(1)} %get-tuple-element.768), channel_id=1, source_target_pairs={{1,0},{2,1},{3,2},{4,3},{5,4},{6,5},{7,6},{8,7},{9,8},{10,9},{11,1... | collective-permute-start | bytes 49160 | tf_op jit(solution)/shard_map/while/body/eval_jaxpr/ppermute | solution.py:22
  479.0 11.0 %collective-permute-start.5 = (f32[1,2,32,128]{3,2,1,0:T(8,128)S(1)}, f32[1,2,32,128]{3,2,1,0:T(8,128)S(1)}, u32[]{:S(2)}, u32[]{:S(2)}) collective-permute-start(f32[1,2,32,128]{3,2,1,0:T(8,128)S(1)} %get-tuple-element.766), channel_id=1, source_target_pairs={{16,0},{32,16},{48,32},{17,1},{33,17},{49,33},{18,2},{34,18},{50,3... | collective-permute-start | bytes 98312 | tf_op jit(solution)/shard_map/while/body/eval_jaxpr/ppermute | solution.py:22
  492.1 8.7 %collective-permute-start.7 = (f32[1,2,64,32]{3,2,1,0:T(8,128)S(1)}, f32[1,2,64,32]{3,2,1,0:T(8,128)S(1)}, u32[]{:S(2)}, u32[]{:S(2)}) collective-permute-start(f32[1,2,64,32]{3,2,1,0:T(8,128)S(1)} %get-tuple-element.768), channel_id=1, source_target_pairs={{1,0},{2,1},{3,2},{4,3},{5,4},{6,5},{7,6},{8,7},{9,8},{10,9},{11,1... | collective-permute-start | bytes 49160 | tf_op jit(solution)/shard_map/while/body/eval_jaxpr/ppermute | solution.py:22
  509.4 11.0 %collective-permute-start.5 = (f32[1,2,32,128]{3,2,1,0:T(8,128)S(1)}, f32[1,2,32,128]{3,2,1,0:T(8,128)S(1)}, u32[]{:S(2)}, u32[]{:S(2)}) collective-permute-start(f32[1,2,32,128]{3,2,1,0:T(8,128)S(1)} %get-tuple-element.766), channel_id=1, source_target_pairs={{16,0},{32,16},{48,32},{17,1},{33,17},{49,33},{18,2},{34,18},{50,3... | collective-permute-start | bytes 98312 | tf_op jit(solution)/shard_map/while/body/eval_jaxpr/ppermute | solution.py:22
  522.5 8.7 %collective-permute-start.7 = (f32[1,2,64,32]{3,2,1,0:T(8,128)S(1)}, f32[1,2,64,32]{3,2,1,0:T(8,128)S(1)}, u32[]{:S(2)}, u32[]{:S(2)}) collective-permute-start(f32[1,2,64,32]{3,2,1,0:T(8,128)S(1)} %get-tuple-element.768), channel_id=1, source_target_pairs={{1,0},{2,1},{3,2},{4,3},{5,4},{6,5},{7,6},{8,7},{9,8},{10,9},{11,1... | collective-permute-start | bytes 49160 | tf_op jit(solution)/shard_map/while/body/eval_jaxpr/ppermute | solution.py:22
  539.6 11.0 %collective-permute-start.5 = (f32[1,2,32,128]{3,2,1,0:T(8,128)S(1)}, f32[1,2,32,128]{3,2,1,0:T(8,128)S(1)}, u32[]{:S(2)}, u32[]{:S(2)}) collective-permute-start(f32[1,2,32,128]{3,2,1,0:T(8,128)S(1)} %get-tuple-element.766), channel_id=1, source_target_pairs={{16,0},{32,16},{48,32},{17,1},{33,17},{49,33},{18,2},{34,18},{50,3... | collective-permute-start | bytes 98312 | tf_op jit(solution)/shard_map/while/body/eval_jaxpr/ppermute | solution.py:22
  552.7 8.7 %collective-permute-start.7 = (f32[1,2,64,32]{3,2,1,0:T(8,128)S(1)}, f32[1,2,64,32]{3,2,1,0:T(8,128)S(1)}, u32[]{:S(2)}, u32[]{:S(2)}) collective-permute-start(f32[1,2,64,32]{3,2,1,0:T(8,128)S(1)} %get-tuple-element.768), channel_id=1, source_target_pairs={{1,0},{2,1},{3,2},{4,3},{5,4},{6,5},{7,6},{8,7},{9,8},{10,9},{11,1... | collective-permute-start | bytes 49160 | tf_op jit(solution)/shard_map/while/body/eval_jaxpr/ppermute | solution.py:22
  569.7 11.0 %collective-permute-start.5 = (f32[1,2,32,128]{3,2,1,0:T(8,128)S(1)}, f32[1,2,32,128]{3,2,1,0:T(8,128)S(1)}, u32[]{:S(2)}, u32[]{:S(2)}) collective-permute-start(f32[1,2,32,128]{3,2,1,0:T(8,128)S(1)} %get-tuple-element.766), channel_id=1, source_target_pairs={{16,0},{32,16},{48,32},{17,1},{33,17},{49,33},{18,2},{34,18},{50,3... | collective-permute-start | bytes 98312 | tf_op jit(solution)/shard_map/while/body/eval_jaxpr/ppermute | solution.py:22
  582.8 8.7 %collective-permute-start.7 = (f32[1,2,64,32]{3,2,1,0:T(8,128)S(1)}, f32[1,2,64,32]{3,2,1,0:T(8,128)S(1)}, u32[]{:S(2)}, u32[]{:S(2)}) collective-permute-start(f32[1,2,64,32]{3,2,1,0:T(8,128)S(1)} %get-tuple-element.768), channel_id=1, source_target_pairs={{1,0},{2,1},{3,2},{4,3},{5,4},{6,5},{7,6},{8,7},{9,8},{10,9},{11,1... | collective-permute-start | bytes 49160 | tf_op jit(solution)/shard_map/while/body/eval_jaxpr/ppermute | solution.py:22
  599.7 11.0 %collective-permute-start.5 = (f32[1,2,32,128]{3,2,1,0:T(8,128)S(1)}, f32[1,2,32,128]{3,2,1,0:T(8,128)S(1)}, u32[]{:S(2)}, u32[]{:S(2)}) collective-permute-start(f32[1,2,32,128]{3,2,1,0:T(8,128)S(1)} %get-tuple-element.766), channel_id=1, source_target_pairs={{16,0},{32,16},{48,32},{17,1},{33,17},{49,33},{18,2},{34,18},{50,3... | collective-permute-start | bytes 98312 | tf_op jit(solution)/shard_map/while/body/eval_jaxpr/ppermute | solution.py:22
  612.9 8.7 %collective-permute-start.7 = (f32[1,2,64,32]{3,2,1,0:T(8,128)S(1)}, f32[1,2,64,32]{3,2,1,0:T(8,128)S(1)}, u32[]{:S(2)}, u32[]{:S(2)}) collective-permute-start(f32[1,2,64,32]{3,2,1,0:T(8,128)S(1)} %get-tuple-element.768), channel_id=1, source_target_pairs={{1,0},{2,1},{3,2},{4,3},{5,4},{6,5},{7,6},{8,7},{9,8},{10,9},{11,1... | collective-permute-start | bytes 49160 | tf_op jit(solution)/shard_map/while/body/eval_jaxpr/ppermute | solution.py:22
  629.8 11.0 %collective-permute-start.5 = (f32[1,2,32,128]{3,2,1,0:T(8,128)S(1)}, f32[1,2,32,128]{3,2,1,0:T(8,128)S(1)}, u32[]{:S(2)}, u32[]{:S(2)}) collective-permute-start(f32[1,2,32,128]{3,2,1,0:T(8,128)S(1)} %get-tuple-element.766), channel_id=1, source_target_pairs={{16,0},{32,16},{48,32},{17,1},{33,17},{49,33},{18,2},{34,18},{50,3... | collective-permute-start | bytes 98312 | tf_op jit(solution)/shard_map/while/body/eval_jaxpr/ppermute | solution.py:22
  643.0 8.7 %collective-permute-start.7 = (f32[1,2,64,32]{3,2,1,0:T(8,128)S(1)}, f32[1,2,64,32]{3,2,1,0:T(8,128)S(1)}, u32[]{:S(2)}, u32[]{:S(2)}) collective-permute-start(f32[1,2,64,32]{3,2,1,0:T(8,128)S(1)} %get-tuple-element.768), channel_id=1, source_target_pairs={{1,0},{2,1},{3,2},{4,3},{5,4},{6,5},{7,6},{8,7},{9,8},{10,9},{11,1... | collective-permute-start | bytes 49160 | tf_op jit(solution)/shard_map/while/body/eval_jaxpr/ppermute | solution.py:22
  659.9 11.0 %collective-permute-start.5 = (f32[1,2,32,128]{3,2,1,0:T(8,128)S(1)}, f32[1,2,32,128]{3,2,1,0:T(8,128)S(1)}, u32[]{:S(2)}, u32[]{:S(2)}) collective-permute-start(f32[1,2,32,128]{3,2,1,0:T(8,128)S(1)} %get-tuple-element.766), channel_id=1, source_target_pairs={{16,0},{32,16},{48,32},{17,1},{33,17},{49,33},{18,2},{34,18},{50,3... | collective-permute-start | bytes 98312 | tf_op jit(solution)/shard_map/while/body/eval_jaxpr/ppermute | solution.py:22
  673.1 8.7 %collective-permute-start.7 = (f32[1,2,64,32]{3,2,1,0:T(8,128)S(1)}, f32[1,2,64,32]{3,2,1,0:T(8,128)S(1)}, u32[]{:S(2)}, u32[]{:S(2)}) collective-permute-start(f32[1,2,64,32]{3,2,1,0:T(8,128)S(1)} %get-tuple-element.768), channel_id=1, source_target_pairs={{1,0},{2,1},{3,2},{4,3},{5,4},{6,5},{7,6},{8,7},{9,8},{10,9},{11,1... | collective-permute-start | bytes 49160 | tf_op jit(solution)/shard_map/while/body/eval_jaxpr/ppermute | solution.py:22
  690.0 11.0 %collective-permute-start.5 = (f32[1,2,32,128]{3,2,1,0:T(8,128)S(1)}, f32[1,2,32,128]{3,2,1,0:T(8,128)S(1)}, u32[]{:S(2)}, u32[]{:S(2)}) collective-permute-start(f32[1,2,32,128]{3,2,1,0:T(8,128)S(1)} %get-tuple-element.766), channel_id=1, source_target_pairs={{16,0},{32,16},{48,32},{17,1},{33,17},{49,33},{18,2},{34,18},{50,3... | collective-permute-start | bytes 98312 | tf_op jit(solution)/shard_map/while/body/eval_jaxpr/ppermute | solution.py:22
  703.1 8.7 %collective-permute-start.7 = (f32[1,2,64,32]{3,2,1,0:T(8,128)S(1)}, f32[1,2,64,32]{3,2,1,0:T(8,128)S(1)}, u32[]{:S(2)}, u32[]{:S(2)}) collective-permute-start(f32[1,2,64,32]{3,2,1,0:T(8,128)S(1)} %get-tuple-element.768), channel_id=1, source_target_pairs={{1,0},{2,1},{3,2},{4,3},{5,4},{6,5},{7,6},{8,7},{9,8},{10,9},{11,1... | collective-permute-start | bytes 49160 | tf_op jit(solution)/shard_map/while/body/eval_jaxpr/ppermute | solution.py:22
  720.1 11.0 %collective-permute-start.5 = (f32[1,2,32,128]{3,2,1,0:T(8,128)S(1)}, f32[1,2,32,128]{3,2,1,0:T(8,128)S(1)}, u32[]{:S(2)}, u32[]{:S(2)}) collective-permute-start(f32[1,2,32,128]{3,2,1,0:T(8,128)S(1)} %get-tuple-element.766), channel_id=1, source_target_pairs={{16,0},{32,16},{48,32},{17,1},{33,17},{49,33},{18,2},{34,18},{50,3... | collective-permute-start | bytes 98312 | tf_op jit(solution)/shard_map/while/body/eval_jaxpr/ppermute | solution.py:22
  733.2 8.7 %collective-permute-start.7 = (f32[1,2,64,32]{3,2,1,0:T(8,128)S(1)}, f32[1,2,64,32]{3,2,1,0:T(8,128)S(1)}, u32[]{:S(2)}, u32[]{:S(2)}) collective-permute-start(f32[1,2,64,32]{3,2,1,0:T(8,128)S(1)} %get-tuple-element.768), channel_id=1, source_target_pairs={{1,0},{2,1},{3,2},{4,3},{5,4},{6,5},{7,6},{8,7},{9,8},{10,9},{11,1... | collective-permute-start | bytes 49160 | tf_op jit(solution)/shard_map/while/body/eval_jaxpr/ppermute | solution.py:22
  750.2 11.0 %collective-permute-start.5 = (f32[1,2,32,128]{3,2,1,0:T(8,128)S(1)}, f32[1,2,32,128]{3,2,1,0:T(8,128)S(1)}, u32[]{:S(2)}, u32[]{:S(2)}) collective-permute-start(f32[1,2,32,128]{3,2,1,0:T(8,128)S(1)} %get-tuple-element.766), channel_id=1, source_target_pairs={{16,0},{32,16},{48,32},{17,1},{33,17},{49,33},{18,2},{34,18},{50,3... | collective-permute-start | bytes 98312 | tf_op jit(solution)/shard_map/while/body/eval_jaxpr/ppermute | solution.py:22
  763.3 8.7 %collective-permute-start.7 = (f32[1,2,64,32]{3,2,1,0:T(8,128)S(1)}, f32[1,2,64,32]{3,2,1,0:T(8,128)S(1)}, u32[]{:S(2)}, u32[]{:S(2)}) collective-permute-start(f32[1,2,64,32]{3,2,1,0:T(8,128)S(1)} %get-tuple-element.768), channel_id=1, source_target_pairs={{1,0},{2,1},{3,2},{4,3},{5,4},{6,5},{7,6},{8,7},{9,8},{10,9},{11,1... | collective-permute-start | bytes 49160 | tf_op jit(solution)/shard_map/while/body/eval_jaxpr/ppermute | solution.py:22
  (87 other events, 872.3 us)
where the time goes:
time: 795 us; the launch traced here: 781 us
  starting transfers between devices  581 us (73%)
  waiting for transfers between devices  169 us (21%)
  matrix products  18.4 us (2%)
    ppermute x52, starting transfers between devices, extended_2(): lax.ppermute(head, axis, [((i + 1) % count, i) for i in range(ends)])  295 us
    ppermute x52, starting transfers between devices, extended_2(): lax.ppermute(tail, axis, [(i, (i + 1) % count) for i in range(ends)])  207 us
    ppermute x52, waiting for transfers between devices, extended_2(): lax.ppermute(tail, axis, [(i, (i + 1) % count) for i in range(ends)])  84.7 us
    ppermute x26, waiting for transfers between devices, from_behind(): lax.ppermute(value, axis, [(source, source + steps) for source in range(l...  84.3 us
    ppermute x26, starting transfers between devices, from_behind(): lax.ppermute(value, axis, [(source, source + steps) for source in range(l...  80 us
  transfers between devices with their start and end apart: 130, of which 78 were waited for; matrix products, arithmetic and copies ran while one was open for 0% of the time, Pallas kernels for 0%

commit v1 on v0

v1 whole, which is shorter than its diff:
```python
import functools
import math

import jax
import jax.numpy as jnp
import numpy as np
from jax import lax
from jax.experimental import pallas as pl
from jax.experimental.pallas import tpu as pltpu
from jax.sharding import PartitionSpec as P

HALO = 32
FRESNEL = 64
WIDTH = 32
MESH = pl.DeviceIdType.MESH
F32 = jnp.float32
BF16 = jnp.bfloat16


def taps(offset):
    offset = offset.astype(np.float64)
    dist = np.maximum(np.abs(offset) - 0.5 * HALO, 0.0)
    profile = np.cos(np.pi * dist / (HALO + 2.0))
    weight = profile * profile / math.sqrt(FRESNEL)
    angle = np.pi * offset * offset / FRESNEL
    inside = np.abs(offset) <= HALO
    re = np.where(inside, np.cos(angle) * weight, 0.0).astype(np.float32)
    im = np.where(inside, np.sin(angle) * weight, 0.0).astype(np.float32)
    return re, im


def halves(matrix):
    high = matrix.astype(BF16)
    low = (matrix - high.astype(np.float32)).astype(BF16)
    return high, low


def matrices(rows):
    i = np.arange(rows)
    re, im = taps(i[None, :] - i[:, None])
    row_high, row_low = halves(np.concatenate([re, im], axis=1))

    out = np.arange(WIDTH)
    blocks = []
    for shift in (-WIDTH, 0, WIDTH):
        re, im = taps(out[:, None] - (out[None, :] + shift))
        blocks.append(np.concatenate([np.concatenate([re, -im], 1), np.concatenate([im, re], 1)], 0))
    mid = np.concatenate(halves(blocks[1]), 0)
    rim = np.concatenate(halves(np.concatenate([blocks[0], blocks[2]], 1)), 0)
    return row_high, row_low, mid, rim


def split(value):
    high = value.astype(BF16)
    return high, (value - high.astype(F32)).astype(BF16)


def dot(a, b):
    return jnp.dot(a, b, preferred_element_type=F32)


def cmul(a, b):
    ar, ai, br, bi = a[:WIDTH], a[WIDTH:], b[:WIDTH], b[WIDTH:]
    return jnp.concatenate([ar * br - ai * bi, ar * bi + ai * br], axis=0)


def kernel(
    depth, cols, y_lo, slices,
    phase, tilt, intensity, row_high, row_low, mid_m, rim_m,
    grad, waves,
    tile_out, tile_in, level_out, level_in, strip_out, phase_w, screens, entering, leaving, moved, halo, grads,
    wave_in, grad_in, wave_out, wave_tiles, grad_out, grad_tiles,
    tile_s, tile_r, level_s, level_r, strip_s, strip_r, halo_s, halo_r, leave_s, leave_r, grads_s, grads_r,
    wave_s, wave_r, gout_s, gout_r,
):
    z, row, col = lax.axis_index("depth"), lax.axis_index("row"), lax.axis_index("col")
    ring = 2 * y_lo
    strips = 4 * cols
    rows = 256
    steps = 2 * slices
    worker = z < 2

    def place(x, turn, core):
        y = turn + (x % 2) * (ring - 1 - 2 * turn)
        return (y // y_lo) * 2 + core, x * y_lo + y % y_lo

    def strip_place(s):
        chip = s // 2
        return place(chip // ring, chip % ring, s % 2)

    x = col // y_lo
    y = (row // 2) * y_lo + col % y_lo
    turn = y + (x % 2) * (ring - 1 - 2 * y)
    strip = 2 * (x * ring + turn) + row % 2
    part = 2 * (turn % 2) + row % 2
    home_col = x * y_lo + turn // 2
    part_places = [place(x, 2 * (col % y_lo) + q // 2, q % 2) for q in range(4)]
    left = strip_place(jnp.maximum(strip - 1, 0))
    right = strip_place(jnp.minimum(strip + 1, strips - 1))
    has_left = worker & (strip > 0)
    has_right = worker & (strip < strips - 1)

    def same(device):
        return (device[0] == z) & (device[1] == row) & (device[2] == col)

    def remote(src, dst, send, recv, device):
        return pltpu.make_async_remote_copy(
            src_ref=src, dst_ref=dst, send_sem=send, recv_sem=recv, device_id=device, device_id_type=MESH
        )

    def push(src, dst, send, recv, device):
        me = same(device)

        @pl.when(jnp.logical_not(me))
        def _():
            remote(src, dst, send, recv, device).start()

        @pl.when(me)
        def _():
            pltpu.make_async_copy(src, dst, recv).start()

    def sent(src, dst, send, recv, device):
        @pl.when(jnp.logical_not(same(device)))
        def _():
            remote(src, dst, send, recv, device).wait_send()

    def arrived(buffer, recv):
        pltpu.make_async_copy(buffer, buffer, recv).wait()

    barrier = pltpu.get_barrier_semaphore()

    def greet(condition, device):
        @pl.when(condition)
        def _():
            pl.semaphore_signal(barrier, inc=1, device_id=device, device_id_type=MESH)

        return condition.astype(jnp.int32)

    expected = jnp.int32(0)
    for q in range(4):
        device = (z,) + part_places[q]
        expected += greet(jnp.logical_not(same(device)), device)
    for r in range(4):
        device = (z, jnp.int32(r), home_col)
        expected += greet(jnp.logical_not(same(device)), device)
    for plane in range(depth):
        wanted = z != plane
        if plane >= 2:
            wanted = wanted & worker
        expected += greet(wanted, (jnp.int32(plane), row, col))
    expected += greet(has_left, (z,) + left)
    expected += greet(has_right, (z,) + right)

    lane = lax.broadcasted_iota(jnp.int32, (16, 128), 1)
    first = lane < 64

    def pack_tile(tile, out):
        turned = jnp.concatenate([tile, tile], axis=0).T
        for q in range(4):
            out[q] = jnp.where(first, turned[32 * q : 32 * q + 16], turned[32 * q + 16 : 32 * q + 32])

    def strip_of(pieces):
        sides = []
        for h in range(2):
            a, b = pieces[2 * h], pieces[2 * h + 1]
            top = jnp.where(first, a, pltpu.roll(b, 64, 1))
            low = jnp.where(first, pltpu.roll(a, 64, 1), b)
            sides.append(jnp.concatenate([top, low], axis=0))
        return jnp.concatenate(sides, axis=1)

    def pack_strip(value, r):
        block = value[:, 128 * (r // 2) : 128 * (r // 2) + 128]
        a, b = block[:16], block[16:]
        if r % 2 == 0:
            return jnp.where(first, a, pltpu.roll(b, 64, 1))
        return jnp.where(first, pltpu.roll(a, 64, 1), b)

    def tile_of(pieces):
        parts = []
        for piece in pieces:
            parts += [piece, pltpu.roll(piece, 64, 1)]
        return jnp.concatenate(parts, axis=0).T[:64]

    pack_tile(phase[0], tile_out)

    @pl.when(worker)
    def _():
        pack_tile(intensity[jnp.minimum(z, 1)], level_out)

    pl.semaphore_wait(barrier, expected)

    for q in range(4):
        push(tile_out.at[q], tile_in.at[row], tile_s.at[q], tile_r, (z,) + part_places[q])

    @pl.when(worker)
    def _():
        for q in range(4):
            push(level_out.at[q], level_in.at[row], level_s.at[q], level_r, (z,) + part_places[q])

    arrived(tile_in, tile_r)
    strip_out[...] = strip_of([tile_in[r] for r in range(4)])
    for b in range(2):
        push(strip_out, phase_w.at[z], strip_s.at[b], strip_r.at[z], (jnp.int32(b), row, col))

    def row_step(value):
        high, low = split(value)
        both = dot(jnp.concatenate([high, low], axis=0), row_high[...])
        full = both[:64] + (both[64:] + dot(high, row_low[...]))
        re = full[:WIDTH, :rows] - full[WIDTH:, rows:]
        im = full[WIDTH:, :rows] + full[:WIDTH, rows:]
        return jnp.concatenate([re, im], axis=0)

    def col_part(matrix, value):
        high, low = split(value)
        both = dot(matrix[...], high)
        return both[:64] + (both[64:] + dot(matrix[:64], low))

    def halo_copies(k):
        return (
            remote(moved.at[k], halo.at[k, pl.ds(64, 64)], halo_s.at[0, k], halo_r.at[1, k], (z,) + left),
            remote(moved.at[k], halo.at[k, pl.ds(0, 64)], halo_s.at[1, k], halo_r.at[0, k], (z,) + right),
        )

    def halo_start(k):
        to_left, to_right = halo_copies(k)
        pl.when(has_left)(to_left.start)
        pl.when(has_right)(to_right.start)

    def halo_wait(k):
        to_left, to_right = halo_copies(k)
        pl.when(has_left)(to_right.wait_recv)
        pl.when(has_right)(to_left.wait_recv)

    def halo_sent(k):
        to_left, to_right = halo_copies(k)
        pl.when(has_left)(to_left.wait_send)
        pl.when(has_right)(to_right.wait_send)

    def make_screen(j):
        arrived(phase_w.at[j], strip_r.at[j])
        angle = phase_w[j]
        screens[j] = jnp.concatenate([jnp.cos(angle), jnp.sin(angle)], axis=0)

    def leave_args(j):
        b = jnp.minimum(z, 1)
        return leaving.at[j], wave_in.at[b], leave_s.at[j], leave_r.at[b], (j, row, col)

    def grads_args(j):
        b = jnp.minimum(z, 1)
        return grads.at[j], grad_in.at[b], grads_s.at[j], grads_r.at[b], (j, row, col)

    @pl.when(worker)
    def _():
        b = jnp.minimum(z, 1)

        @pl.when(strip == 0)
        def _():
            @pl.loop(0, steps)
            def _(k):
                halo[k, pl.ds(0, 64)] = jnp.zeros((64, rows), F32)

        @pl.when(strip == strips - 1)
        def _():
            @pl.loop(0, steps)
            def _(k):
                halo[k, pl.ds(64, 64)] = jnp.zeros((64, rows), F32)

        shape = (WIDTH, rows)
        row_pos = lax.broadcasted_iota(jnp.int32, shape, 1).astype(F32)
        col_pos = (strip * WIDTH + lax.broadcasted_iota(jnp.int32, shape, 0)).astype(F32)
        t0, t1 = tilt[b, 0].astype(F32), tilt[b, 1].astype(F32)
        angle = 2.0 * jnp.pi * (t0 * row_pos / float(rows) + t1 * col_pos / float(strips * WIDTH))
        incident = jnp.concatenate([jnp.cos(angle), jnp.sin(angle)], axis=0)
        make_screen(0)
        start = cmul(screens[0], incident)
        entering[0] = start
        moved[0] = row_step(start)

        def forward(j, carry):
            halo_start(j)
            local = col_part(mid_m, moved[j])

            @pl.when(j > 0)
            def _():
                push(*leave_args(j - 1))

            make_screen(j + 1)
            halo_wait(j)
            wave = local + col_part(rim_m, halo[j])
            leaving[j] = wave
            after = cmul(screens[j + 1], wave)
            entering[j + 1] = after
            moved[j + 1] = row_step(after)
            return carry

        lax.fori_loop(0, slices - 1, forward, 0)

        last = slices - 1
        halo_start(last)
        local = col_part(mid_m, moved[last])
        if last > 0:
            push(*leave_args(jnp.int32(last - 1)))
        arrived(level_in, level_r)
        level = strip_of([level_in[r] for r in range(4)])
        halo_wait(last)
        wave = local + col_part(rim_m, halo[last])
        leaving[last] = wave
        re, im = wave[:WIDTH], wave[WIDTH:]
        misfit = 2.0 * (re * re + im * im - level)
        moved[slices] = row_step(jnp.concatenate([misfit * re, -(misfit * im)], axis=0))
        halo_start(slices)
        push(*leave_args(jnp.int32(last)))

        def gradient(j, pulled):
            source = entering[j]
            grads[j] = -(pulled[:WIDTH] * source[WIDTH:] + pulled[WIDTH:] * source[:WIDTH])

        def backward(k, carry):
            j = steps - 1 - k
            local = col_part(mid_m, moved[k])
            halo_wait(k)
            pulled = local + col_part(rim_m, halo[k])
            moved[k + 1] = row_step(cmul(screens[j], pulled))
            halo_start(k + 1)
            gradient(j, pulled)
            push(*grads_args(j))
            return carry

        lax.fori_loop(slices, steps - 1, backward, 0)
        local = col_part(mid_m, moved[steps - 1])
        halo_wait(steps - 1)
        gradient(0, local + col_part(rim_m, halo[steps - 1]))
        push(*grads_args(jnp.int32(0)))

    for b in range(2):
        arrived(wave_in.at[b], leave_r.at[b])
        for r in range(4):
            for c in range(2):
                wave_out[b, r, c] = pack_strip(wave_in[b, pl.ds(32 * c, 32)], r)
            push(wave_out.at[b, r], wave_tiles.at[b, part], wave_s.at[b, r], wave_r.at[b], (z, jnp.int32(r), home_col))
    for b in range(2):
        arrived(wave_tiles.at[b], wave_r.at[b])
        for c in range(2):
            waves[b, 0, c] = tile_of([wave_tiles[b, q, c] for q in range(4)])
    for b in range(2):
        arrived(grad_in.at[b], grads_r.at[b])
    total = grad_in[0] + grad_in[1]
    for r in range(4):
        grad_out[r] = pack_strip(total, r)
        push(grad_out.at[r], grad_tiles.at[part], gout_s.at[r], gout_r, (z, jnp.int32(r), home_col))
    arrived(grad_tiles, gout_r)
    grad[0] = tile_of([grad_tiles[q] for q in range(4)])

    for q in range(4):
        sent(tile_out.at[q], tile_in.at[row], tile_s.at[q], tile_r, (z,) + part_places[q])
        sent(grad_out.at[q], grad_tiles.at[part], gout_s.at[q], gout_r, (z, jnp.int32(q), home_col))
        for b in range(2):
            sent(wave_out.at[b, q], wave_tiles.at[b, part], wave_s.at[b, q], wave_r.at[b], (z, jnp.int32(q), home_col))
    for b in range(2):
        sent(strip_out, phase_w.at[z], strip_s.at[b], strip_r.at[z], (jnp.int32(b), row, col))

    @pl.when(worker)
    def _():
        for q in range(4):
            sent(level_out.at[q], level_in.at[row], level_s.at[q], level_r, (z,) + part_places[q])

        @pl.loop(0, steps)
        def _(k):
            halo_sent(k)

        @pl.loop(0, slices)
        def _(j):
            sent(*leave_args(j))
            sent(*grads_args(j))


def solution(mesh):
    depth, cols = mesh.shape["depth"], mesh.shape["col"]
    y_lo = 4 if cols % 4 == 0 else 1
    slices = depth
    steps = 2 * slices
    rows = 256
    constants = [jnp.asarray(m) for m in matrices(rows)]

    def body(phase, tilt, intensity):
        vmem = pl.BlockSpec(memory_space=pltpu.VMEM)
        dma = pltpu.SemaphoreType.DMA
        wave = (64, rows)
        flops = 2 * steps * 64 * rows * (3 * 512 + 3 * 192)
        return pl.pallas_call(
            functools.partial(kernel, depth, cols, y_lo, slices),
            out_shape=(
                jax.ShapeDtypeStruct((1, 64, 128), F32),
                jax.ShapeDtypeStruct((2, 1, 2, 64, 128), F32),
            ),
            in_specs=[vmem, pl.BlockSpec(memory_space=pltpu.SMEM)] + [vmem] * 5,
            out_specs=(vmem, vmem),
            scratch_shapes=[
                pltpu.VMEM((4, 16, 128), F32),
                pltpu.VMEM((4, 16, 128), F32),
                pltpu.VMEM((4, 16, 128), F32),
                pltpu.VMEM((4, 16, 128), F32),
                pltpu.VMEM((WIDTH, rows), F32),
                pltpu.VMEM((slices, WIDTH, rows), F32),
                pltpu.VMEM((slices,) + wave, F32),
                pltpu.VMEM((slices,) + wave, F32),
                pltpu.VMEM((slices,) + wave, F32),
                pltpu.VMEM((steps,) + wave, F32),
                pltpu.VMEM((steps, 128, rows), F32),
                pltpu.VMEM((slices, WIDTH, rows), F32),
                pltpu.VMEM((2,) + wave, F32),
                pltpu.VMEM((2, WIDTH, rows), F32),
                pltpu.VMEM((2, 4, 2, 16, 128), F32),
                pltpu.VMEM((2, 4, 2, 16, 128), F32),
                pltpu.VMEM((4, 16, 128), F32),
                pltpu.VMEM((4, 16, 128), F32),
                dma((4,)),
                dma,
                dma((4,)),
                dma,
                dma((2,)),
                dma((slices,)),
                dma((2, steps)),
                dma((2, steps)),
                dma((slices,)),
                dma((2,)),
                dma((slices,)),
                dma((2,)),
                dma((2, 4)),
                dma((2,)),
                dma((4,)),
                dma,
            ],
            compiler_params=pltpu.CompilerParams(
                collective_id=0, has_side_effects=True, vmem_limit_bytes=48 * 2**20
            ),
            cost_estimate=pl.CostEstimate(flops=flops, bytes_accessed=2**21, transcendentals=2**18),
        )(phase, tilt, intensity, *constants)

    placed = (P("depth", "row", "col"), P(), P(None, "row", "col"))
    return jax.shard_map(
        body,
        mesh=mesh,
        in_specs=placed,
        out_specs=(P("depth", "row", "col"), P(None, "depth", None, "row", "col")),
        check_vma=False,
    )
```

time: 795 us -> 136 us (0.17)
  the two profiles are of different devices: /device:TPU:57 before, /device:TPU:71 now
where the time goes in v1:
time: 136 us; the launch traced here: 135 us
  Pallas kernels  128 us (94%)
  local copies, waits for them, and re-layouts  6.95 us (5%)
    pallas_call x1, Pallas kernels, body(): pl.pallas_call(functools.partial(kernel, depth, cols, y_lo, slices), out_...  128 us
    unnamed x16, local copies, waits for them, and re-layouts  6.95 us

profile of v1, /device:TPU:71, one launch (start us, length us, event | category | flops | bytes accessed | tf_op | source)
XLA Modules:
  0.0 135.3 jit_solution(2876908777260331460)
XLA Ops:
  0.6 0.0 copy-start
  0.6 0.8 copy-done
  1.5 0.0 copy-start.1
  1.5 0.8 copy-done.1
  2.2 0.0 copy-start.2
  2.2 0.7 copy-done.2
  2.9 0.0 copy-start.3
  2.9 0.9 copy-done.3
  3.9 0.0 copy-start.4
  3.9 0.9 copy-done.4
  4.8 0.0 copy-start.5
  4.8 0.8 copy-done.5
  5.6 0.0 copy-start.6
  5.6 0.8 copy-done.6
  6.3 127.7 %shard_map.86 = (f32[1,64,128]{2,1,0:T(8,128)S(1)}, f32[2,1,2,64,128]{4,3,2,1,0:T(8,128)S(1)}) custom-call(f32[1,64,128]{2,1,0:T(8,128)S(1)} %copy-done.1, s32[2,2]{1,0:T(2,128)S(1)} %copy-done.2, f32[2,64,128]{2,1,0:T(8,128)S(1)} %copy-done, bf16[256,512]{1,0:T(8,128)(2,1)S(1)} %copy-done.4, bf16[256,512]{1,0:T(8,128)(2,1)S(1)} %copy-done.3, ...), custom_call_target="tpu_custom_call" | custom-call | flops 1660944384 | bytes 2097152 | tf_op jit(solution)/shard_map/pallas_call | solution.py:390
  134.0 0.6 copy.11
  134.6 0.7 copy.12
Async XLA Ops:
  0.6 0.8 copy-start
  1.5 0.8 copy-start.1
  2.2 0.7 copy-start.2
  2.9 0.9 copy-start.3
  3.9 0.9 copy-start.4
  4.8 0.8 copy-start.5
  5.6 0.8 copy-start.6

commit v2 on v1

v2 whole, which is shorter than its diff:
```python
import functools
import math

import jax
import jax.numpy as jnp
import numpy as np
from jax import lax
from jax.experimental import pallas as pl
from jax.experimental.pallas import tpu as pltpu
from jax.sharding import PartitionSpec as P

HALO = 32
FRESNEL = 64
WIDTH = 32
OWN = 4
RUN = 4
ROWS = 256
MESH = pl.DeviceIdType.MESH
F32 = jnp.float32
BF16 = jnp.bfloat16


def taps(offset):
    offset = offset.astype(np.float64)
    dist = np.maximum(np.abs(offset) - 0.5 * HALO, 0.0)
    profile = np.cos(np.pi * dist / (HALO + 2.0))
    weight = profile * profile / math.sqrt(FRESNEL)
    angle = np.pi * offset * offset / FRESNEL
    inside = np.abs(offset) <= HALO
    re = np.where(inside, np.cos(angle) * weight, 0.0).astype(np.float32)
    im = np.where(inside, np.sin(angle) * weight, 0.0).astype(np.float32)
    return re, im


def halves(matrix):
    high = matrix.astype(BF16)
    low = (matrix - high.astype(np.float32)).astype(BF16)
    return high, low


def matrices():
    i = np.arange(ROWS)
    re, im = taps(i[None, :] - i[:, None])
    row_high, row_low = halves(np.concatenate([re, im], axis=1))

    lines = []
    for o in range(2):
        out = WIDTH * o + np.arange(WIDTH)
        top, low = [], []
        for i in range(4):
            re, im = taps(out[:, None] - (WIDTH * (i - 1) + np.arange(WIDTH))[None, :])
            top += [re, -im]
            low += [im, re]
        lines += [np.concatenate(top, 1), np.concatenate(low, 1)]
    pair = np.concatenate(halves(np.concatenate(lines, 0)), 0)
    return row_high, row_low, pair


def split(value):
    high = value.astype(BF16)
    return high, (value - high.astype(F32)).astype(BF16)


def dot(a, b):
    return jnp.dot(a, b, preferred_element_type=F32)


def blocks_of(value):
    for g in range(value.shape[0] // 64):
        yield value[64 * g : 64 * g + 32], value[64 * g + 32 : 64 * g + 64]


def cmul(a, b):
    out = []
    for (ar, ai), (br, bi) in zip(blocks_of(a), blocks_of(b)):
        out += [ar * br - ai * bi, ar * bi + ai * br]
    return jnp.concatenate(out, axis=0)


def cos_sin(x):
    y = x * x
    c = F32(-1.0 / math.factorial(14))
    s = F32(-1.0 / math.factorial(15))
    for n in range(6, -1, -1):
        sign = -1.0 if n % 2 else 1.0
        c = c * y + F32(sign / math.factorial(2 * n))
        s = s * y + F32(sign / math.factorial(2 * n + 1))
    return c, s * x


def kernel(
    depth, cols, y_lo, slices,
    phase_h, tilt_h, intensity_h, row_high_h, row_low_h, pair_h,
    grad, waves,
    phase, tilt, intensity, row_high, row_low, pair,
    tiles_in, levels_in, wide_out, phase_w, screens, entering, leaving, spread, work, grads,
    wave_in, grad_in, wave_out, grad_out, grad_tiles,
    load_s, tile_s, tile_r, level_s, level_r, wide_s, wide_r, halo_s, halo_r, leave_s, wave_r, grads_s, gin_r,
    wout_s, wout_r, gout_s, gout_r,
):
    z, row, col = lax.axis_index("depth"), lax.axis_index("row"), lax.axis_index("col")
    ring = 2 * y_lo
    half = cols // ring
    rounds = slices // RUN
    rim = RUN - 1
    own_rows = 64 * OWN
    side = 64 * RUN

    loads = [
        pltpu.make_async_copy(src, dst, load_s.at[i])
        for i, (src, dst) in enumerate(
            (
                (phase_h, phase), (intensity_h, intensity), (tilt_h, tilt),
                (row_high_h, row_high), (row_low_h, row_low), (pair_h, pair),
            )
        )
    ]
    for load in loads:
        load.start()

    x = col // y_lo
    y = (row // 2) * y_lo + col % y_lo
    b = x // half
    place_x = x % half
    strip = place_x * ring + y + (place_x % 2) * (ring - 1 - 2 * y)
    hub = row % 2 == 0
    worker = hub & (z == 0)
    wide = z % RUN != 0

    def hub_place(tilt_index, s):
        sx = s // ring
        turn = s % ring
        hy = turn + (sx % 2) * (ring - 1 - 2 * turn)
        return (hy // y_lo) * 2, (tilt_index * half + sx) * y_lo + hy % y_lo

    def clamp(s):
        return jnp.minimum(jnp.maximum(s, 0), cols - 1)

    left = (z,) + hub_place(b, clamp(strip - 1))
    right = (z,) + hub_place(b, clamp(strip + 1))
    has_left = worker & (strip > 0)
    has_right = worker & (strip < cols - 1)

    def same(device):
        return (device[0] == z) & (device[1] == row) & (device[2] == col)

    def remote(src, dst, send, recv, device):
        return pltpu.make_async_remote_copy(
            src_ref=src, dst_ref=dst, send_sem=send, recv_sem=recv, device_id=device, device_id_type=MESH
        )

    def push(src, dst, send, recv, device):
        me = same(device)

        @pl.when(jnp.logical_not(me))
        def _():
            remote(src, dst, send, recv, device).start()

        @pl.when(me)
        def _():
            pltpu.make_async_copy(src, dst, recv).start()

    def sent(src, dst, send, recv, device):
        @pl.when(jnp.logical_not(same(device)))
        def _():
            remote(src, dst, send, recv, device).wait_send()

    def arrived(buffer, recv):
        pltpu.make_async_copy(buffer, buffer, recv).wait()

    def tile_hubs():
        for t in range(2):
            for d in range(3):
                s = col + 1 - d
                wanted = (s >= 0) & (s < cols)
                if d != 1:
                    wanted = wanted & wide
                yield t, d, wanted, (z,) + hub_place(t, clamp(s))

    def hub_tiles():
        for d in range(3):
            c = strip + d - 1
            wanted = hub & (c >= 0) & (c < cols)
            if d != 1:
                wanted = wanted & wide
            for r in range(4):
                yield wanted, (z, jnp.int32(r), clamp(c))

    barrier = pltpu.get_barrier_semaphore()

    def greet(condition, device):
        @pl.when(condition)
        def _():
            pl.semaphore_signal(barrier, inc=1, device_id=device, device_id_type=MESH)

        return condition.astype(jnp.int32)

    expected = jnp.int32(0)
    for _, _, wanted, device in tile_hubs():
        expected += greet(wanted & jnp.logical_not(same(device)), device)
    for wanted, device in hub_tiles():
        expected += greet(wanted & jnp.logical_not(same(device)), device)
    for plane in range(1, depth):
        expected += greet(worker, (jnp.int32(plane), row, col))
    expected += greet(hub & (z != 0), (jnp.int32(0), row, col))
    expected += greet(has_left, left)
    expected += greet(has_right, right)

    loads[0].wait()
    loads[1].wait()
    pl.semaphore_wait(barrier, expected)

    for t, d, wanted, device in tile_hubs():
        pl.when(wanted)(
            functools.partial(push, phase.at[0], tiles_in.at[d, row], tile_s.at[t, d], tile_r.at[d], device)
        )

    def level_args(t):
        return intensity.at[t], levels_in.at[row], level_s.at[t], level_r, (z,) + hub_place(t, col)

    @pl.when(z == 0)
    def _():
        for t in range(2):
            push(*level_args(t))

    def turn_tiles(tiles, h):
        return jnp.concatenate([tiles[2 * h], tiles[2 * h + 1]], axis=0).T

    def wide_copy():
        return remote(wide_out, phase_w.at[z], wide_s, wide_r.at[z], (jnp.int32(0), row, col))

    def own_copy():
        span = pl.ds(32 * rim, 32 * OWN)
        return remote(wide_out.at[span], phase_w.at[z, span], wide_s, wide_r.at[z], (jnp.int32(0), row, col))

    @pl.when(hub)
    def _():
        arrived(tiles_in.at[1], tile_r.at[1])

        @pl.when(worker)
        def _():
            for h in range(2):
                phase_w[0, 32 * rim : 32 * (rim + OWN), 128 * h : 128 * h + 128] = turn_tiles(tiles_in[1], h)

        @pl.when(z != 0)
        def _():
            for h in range(2):
                wide_out[32 * rim : 32 * (rim + OWN), 128 * h : 128 * h + 128] = turn_tiles(tiles_in[1], h)

            @pl.when(wide)
            def _():
                @pl.when(strip > 0)
                def _():
                    arrived(tiles_in.at[0], tile_r.at[0])
                    for h in range(2):
                        turned = turn_tiles(tiles_in[0], h)
                        wide_out[: 32 * rim, 128 * h : 128 * h + 128] = turned[128 - 32 * rim :]

                @pl.when(strip == 0)
                def _():
                    wide_out[: 32 * rim] = jnp.zeros((32 * rim, ROWS), F32)

                @pl.when(strip < cols - 1)
                def _():
                    arrived(tiles_in.at[2], tile_r.at[2])
                    for h in range(2):
                        turned = turn_tiles(tiles_in[2], h)
                        wide_out[32 * (rim + OWN) :, 128 * h : 128 * h + 128] = turned[: 32 * rim]

                @pl.when(strip == cols - 1)
                def _():
                    wide_out[32 * (rim + OWN) :] = jnp.zeros((32 * rim, ROWS), F32)

                wide_copy().start()

            @pl.when(jnp.logical_not(wide))
            def _():
                own_copy().start()

    for load in loads[2:]:
        load.wait()

    def row_step(value):
        high, low = split(value)
        full = dot(high, row_high[...]) + (dot(low, row_high[...]) + dot(high, row_low[...]))
        out = []
        for a, c in blocks_of(full):
            out += [a[:, :ROWS] - c[:, ROWS:], c[:, :ROWS] + a[:, ROWS:]]
        return jnp.concatenate(out, axis=0)

    def col_step(value):
        high, low = split(value)
        out = []
        for p in range(value.shape[0] // 128 - 1):
            h, l = high[128 * p : 128 * p + 256], low[128 * p : 128 * p + 256]
            both = dot(pair[...], h)
            out.append(both[:128] + (both[128:] + dot(pair[:128], l)))
        return jnp.concatenate(out, axis=0)

    def halo_copies(k):
        return (
            remote(
                spread.at[k, pl.ds(side, side)], spread.at[k, pl.ds(side + own_rows, side)],
                halo_s.at[0, k], halo_r.at[1, k], left,
            ),
            remote(
                spread.at[k, pl.ds(own_rows, side)], spread.at[k, pl.ds(0, side)],
                halo_s.at[1, k], halo_r.at[0, k], right,
            ),
        )

    def halo_start(k):
        to_left, to_right = halo_copies(k)
        pl.when(has_left)(to_left.start)
        pl.when(has_right)(to_right.start)

    def halo_wait(k):
        to_left, to_right = halo_copies(k)
        pl.when(has_left)(to_right.wait_recv)
        pl.when(has_right)(to_left.wait_recv)

    def halo_sent(k):
        to_left, to_right = halo_copies(k)
        pl.when(has_left)(to_left.wait_send)
        pl.when(has_right)(to_right.wait_send)

    def make_screen(j, with_rim):
        for g in range(0 if with_rim else rim, OWN + (2 * rim if with_rim else rim)):
            c, s = cos_sin(phase_w[j, 32 * g : 32 * g + 32])
            if g < rim:
                c, s = jnp.where(strip > 0, c, 0.0), jnp.where(strip > 0, s, 0.0)
            if g >= rim + OWN:
                c, s = jnp.where(strip < cols - 1, c, 0.0), jnp.where(strip < cols - 1, s, 0.0)
            screens[j, 64 * g : 64 * g + 32] = c
            screens[j, 64 * g + 32 : 64 * g + 64] = s

    def get_screen(j, with_rim):
        if with_rim:
            arrived(phase_w.at[j], wide_r.at[j])
        else:
            span = pl.ds(32 * rim, 32 * OWN)
            arrived(phase_w.at[j, span], wide_r.at[j])
        make_screen(j, with_rim)

    def screen_on(j, out):
        return screens[j, pl.ds(64 * (rim - out), 64 * (OWN + 2 * out))]

    def leave_args(j):
        return leaving.at[j], wave_in, leave_s.at[j], wave_r, (j, row, col)

    def grads_args(j):
        return grads.at[j], grad_in, grads_s.at[j], gin_r, (j, row, col)

    def leave_start(j):
        pl.when(j > 0)(remote(*leave_args(j)).start)

    def grads_start(j):
        pl.when(j > 0)(remote(*grads_args(j)).start)

    def wave_turn(src):
        for c in range(2):
            value = jnp.concatenate([src[64 * g + 32 * c : 64 * g + 32 * c + 32] for g in range(OWN)], axis=0)
            for h in range(2):
                turned = value[:, 128 * h : 128 * h + 128].T
                wave_out[2 * h, c] = turned[:64]
                wave_out[2 * h + 1, c] = turned[64:]
        for r in range(4):
            push(*wave_args(r))

    def wave_args(r):
        return wave_out.at[r], waves.at[b, 0], wout_s.at[r], wout_r.at[b], (z, jnp.int32(r), strip)

    def grad_turn(src):
        for h in range(2):
            turned = src[:, 128 * h : 128 * h + 128].T
            grad_out[2 * h] = turned[:64]
            grad_out[2 * h + 1] = turned[64:]
        for r in range(4):
            push(*grad_args(r))

    def grad_args(r):
        return grad_out.at[r], grad_tiles.at[b], gout_s.at[r], gout_r.at[b], (z, jnp.int32(r), strip)

    def next_input(i, k):
        return spread[k] if i == 1 else work[pl.ds(0, 64 * (OWN + 2 * (RUN - i + 1)))]

    def own_part(value, out):
        return value[64 * out : 64 * out + own_rows]

    def forward(k, last):
        first_slice = k * RUN
        halo_start(k)
        for i in range(1, RUN + (0 if last else 1)):
            get_screen(first_slice + i, i < RUN)
        halo_wait(k)
        for i in range(1, RUN + 1):
            out = RUN - i
            j = first_slice + i - 1
            wave = col_step(next_input(i, k))
            leaving[j] = own_part(wave, out)
            leave_start(j)
            if i < RUN:
                after = cmul(screen_on(j + 1, out), wave)
                entering[j + 1] = own_part(after, out)
                work[pl.ds(0, 64 * (OWN + 2 * out))] = row_step(after)
            elif not last:
                after = cmul(screen_on(j + 1, 0), wave)
                entering[j + 1] = after
                spread[k + 1, pl.ds(side, own_rows)] = row_step(after)
            else:
                arrived(levels_in, level_r)
                level = jnp.concatenate([turn_tiles(levels_in, h) for h in range(2)], axis=1)
                seed = []
                for g, (re, im) in enumerate(blocks_of(wave)):
                    misfit = 2.0 * (re * re + im * im - level[32 * g : 32 * g + 32])
                    seed += [misfit * re, -(misfit * im)]
                spread[k + 1, pl.ds(side, own_rows)] = row_step(jnp.concatenate(seed, axis=0))

    def backward(k, last):
        first_slice = (2 * rounds - k) * RUN - 1
        halo_wait(k)
        for i in range(1, RUN + 1):
            out = RUN - i
            j = first_slice - (i - 1)
            pulled = col_step(next_input(i, k))
            if i < RUN:
                work[pl.ds(0, 64 * (OWN + 2 * out))] = row_step(cmul(screen_on(j, out), pulled))
            elif not last:
                spread[k + 1, pl.ds(side, own_rows)] = row_step(cmul(screen_on(j, 0), pulled))
                halo_start(k + 1)
            parts = []
            for (pr, pi), (er, ei) in zip(blocks_of(own_part(pulled, out)), blocks_of(entering[j])):
                parts.append(-(pr * ei + pi * er))
            grads[j] = jnp.concatenate(parts, axis=0)
            grads_start(j)

    @pl.when(worker)
    def _():
        @pl.when(strip == 0)
        def _():
            @pl.loop(0, 2 * rounds)
            def _(k):
                spread[k, pl.ds(0, side)] = jnp.zeros((side, ROWS), F32)

        @pl.when(strip == cols - 1)
        def _():
            @pl.loop(0, 2 * rounds)
            def _(k):
                spread[k, pl.ds(side + own_rows, side)] = jnp.zeros((side, ROWS), F32)

        row_pos = lax.broadcasted_iota(jnp.int32, (32 * OWN, ROWS), 1).astype(F32)
        col_pos = (strip * (32 * OWN) + lax.broadcasted_iota(jnp.int32, (32 * OWN, ROWS), 0)).astype(F32)
        t0, t1 = tilt[b, 0].astype(F32), tilt[b, 1].astype(F32)
        angle = 2.0 * jnp.pi * (t0 * row_pos / float(ROWS) + t1 * col_pos / float(cols * 32 * OWN))
        cos, sin = jnp.cos(angle), jnp.sin(angle)
        incident = []
        for g in range(OWN):
            incident += [cos[32 * g : 32 * g + 32], sin[32 * g : 32 * g + 32]]
        make_screen(0, False)
        start = cmul(screen_on(0, 0), jnp.concatenate(incident, axis=0))
        entering[0] = start
        spread[0, pl.ds(side, own_rows)] = row_step(start)

        def forward_round(k, carry):
            forward(k, False)
            return carry

        def backward_round(k, carry):
            backward(k, False)
            return carry

        if rounds > 1:
            lax.fori_loop(0, rounds - 1, forward_round, 0)
        forward(jnp.int32(rounds - 1), True)
        halo_start(rounds)
        wave_turn(leaving.at[0])
        if rounds > 1:
            lax.fori_loop(rounds, 2 * rounds - 1, backward_round, 0)
        backward(jnp.int32(2 * rounds - 1), True)
        grad_turn(grads.at[0])

    @pl.when(hub & (z != 0))
    def _():
        arrived(wave_in, wave_r)
        wave_turn(wave_in)
        arrived(grad_in, gin_r)
        grad_turn(grad_in)

    for t in range(2):
        arrived(waves.at[t, 0], wout_r.at[t])
    for t in range(2):
        arrived(grad_tiles.at[t], gout_r.at[t])
    grad[0] = grad_tiles[0] + grad_tiles[1]

    for t, d, wanted, device in tile_hubs():
        pl.when(wanted)(
            functools.partial(sent, phase.at[0], tiles_in.at[d, row], tile_s.at[t, d], tile_r.at[d], device)
        )

    @pl.when(z == 0)
    def _():
        for t in range(2):
            sent(*level_args(t))

    @pl.when(hub)
    def _():
        for r in range(4):
            sent(*wave_args(r))
            sent(*grad_args(r))
        pl.when((z != 0) & wide)(wide_copy().wait_send)
        pl.when((z != 0) & jnp.logical_not(wide))(own_copy().wait_send)

    @pl.when(worker)
    def _():
        @pl.loop(0, 2 * rounds)
        def _(k):
            halo_sent(k)

        @pl.loop(1, slices)
        def _(j):
            remote(*leave_args(j)).wait_send()
            remote(*grads_args(j)).wait_send()


def solution(mesh):
    depth, cols = mesh.shape["depth"], mesh.shape["col"]
    y_lo = 4 if cols % 8 == 0 else 1
    slices = depth
    rounds = 2 * slices // RUN
    reach = OWN + 2 * (RUN - 1)
    constants = [jnp.asarray(m) for m in matrices()]

    def body(phase, tilt, intensity):
        hbm = pl.BlockSpec(memory_space=pltpu.HBM)
        vmem = pl.BlockSpec(memory_space=pltpu.VMEM)
        dma = pltpu.SemaphoreType.DMA
        strip = (64 * OWN, ROWS)
        flops = 2 * 2 * slices * 64 * 7 * ROWS * (3 * 512 + 3 * 256)
        return pl.pallas_call(
            functools.partial(kernel, depth, cols, y_lo, slices),
            out_shape=(
                jax.ShapeDtypeStruct((1, 64, 128), F32),
                jax.ShapeDtypeStruct((2, 1, 2, 64, 128), F32),
            ),
            in_specs=[hbm] * 6,
            out_specs=(vmem, vmem),
            scratch_shapes=[
                pltpu.VMEM((1, 64, 128), F32),
                pltpu.SMEM((2, 2), jnp.int32),
                pltpu.VMEM((2, 64, 128), F32),
                pltpu.VMEM((ROWS, 2 * ROWS), BF16),
                pltpu.VMEM((ROWS, 2 * ROWS), BF16),
                pltpu.VMEM((256, 256), BF16),
                pltpu.VMEM((3, 4, 64, 128), F32),
                pltpu.VMEM((4, 64, 128), F32),
                pltpu.VMEM((32 * reach, ROWS), F32),
                pltpu.VMEM((slices, 32 * reach, ROWS), F32),
                pltpu.VMEM((slices, 64 * reach, ROWS), F32),
                pltpu.VMEM((slices,) + strip, F32),
                pltpu.VMEM((slices,) + strip, F32),
                pltpu.VMEM((rounds, 64 * (OWN + 2 * RUN), ROWS), F32),
                pltpu.VMEM((64 * reach, ROWS), F32),
                pltpu.VMEM((slices, 32 * OWN, ROWS), F32),
                pltpu.VMEM(strip, F32),
                pltpu.VMEM((32 * OWN, ROWS), F32),
                pltpu.VMEM((4, 2, 64, 128), F32),
                pltpu.VMEM((4, 64, 128), F32),
                pltpu.VMEM((2, 64, 128), F32),
                dma((6,)),
                dma((2, 3)),
                dma((3,)),
                dma((2,)),
                dma,
                dma,
                dma((slices,)),
                dma((2, rounds)),
                dma((2, rounds)),
                dma((slices,)),
                dma,
                dma((slices,)),
                dma,
                dma((4,)),
                dma((2,)),
                dma((4,)),
                dma((2,)),
            ],
            compiler_params=pltpu.CompilerParams(
                collective_id=0, has_side_effects=True, vmem_limit_bytes=56 * 2**20
            ),
            cost_estimate=pl.CostEstimate(flops=flops, bytes_accessed=2**21, transcendentals=2**18),
        )(phase, tilt, intensity, *constants)

    placed = (P("depth", "row", "col"), P(), P(None, "row", "col"))
    return jax.shard_map(
        body,
        mesh=mesh,
        in_specs=placed,
        out_specs=(P("depth", "row", "col"), P(None, "depth", None, "row", "col")),
        check_vma=False,
    )
```

time: 136 us -> 115 us (0.85)
  the two profiles are of different devices: /device:TPU:71 before, /device:TPU:67 now
where the time goes in v2:
time: 115 us
  Pallas kernels  111 us (97%)
  local copies, waits for them, and re-layouts  2.94 us (3%)
    pallas_call x1, Pallas kernels, body(): pl.pallas_call(functools.partial(kernel, depth, cols, y_lo, slices), out_...  111 us
    unnamed x2, local copies, waits for them, and re-layouts  2.94 us

profile of v2, /device:TPU:67, one launch (start us, length us, event | category | flops | bytes accessed | tf_op | source)
XLA Modules:
  0.0 114.6 jit_solution(1273746298422070883)
XLA Ops:
  0.6 111.1 %shard_map.77 = (f32[1,64,128]{2,1,0:T(8,128)}, f32[2,1,2,64,128]{4,3,2,1,0:T(8,128)}) custom-call(f32[1,64,128]{2,1,0:T(8,128)} %phase_h.1, s32[2,2]{1,0:T(2,128)} %tilt_h.1, f32[2,64,128]{2,1,0:T(8,128)} %intensity_h.1, bf16[256,512]{1,0:T(8,128)(2,1)} %constant.6.clone.row_high_h, bf16[256,512]{1,0:T(8,128)(2,1)} %constant.7.clone.row_low_h, ...), custom_call_target="tpu_custom_call" | custom-call | flops 12683575296 | bytes 2097152 | tf_op jit(solution)/shard_map/pallas_call | solution.py:539
  111.7 1.4 %copy.10 = f32[1,64,128]{2,1,0:T(8,128)} copy(f32[1,64,128]{2,1,0:T(8,128)} %get-tuple-element.4) | data formatting | bytes 65536
  113.1 1.6 %copy.11 = f32[2,1,2,64,128]{4,3,2,1,0:T(8,128)} copy(f32[2,1,2,64,128]{4,3,2,1,0:T(8,128)} %get-tuple-element.5) | data formatting | bytes 262144

commit v3 on v2

--- a/solution.py
+++ b/solution.py
@@ -15,6 +15,7 @@
 OWN = 4
 RUN = 4
 ROWS = 256
+HOME = 2
 MESH = pl.DeviceIdType.MESH
 F32 = jnp.float32
 BF16 = jnp.bfloat16
@@ -95,8 +96,8 @@
     phase, tilt, intensity, row_high, row_low, pair,
     tiles_in, levels_in, wide_out, phase_w, screens, entering, leaving, spread, work, grads,
     wave_in, grad_in, wave_out, grad_out, grad_tiles,
-    load_s, tile_s, tile_r, level_s, level_r, wide_s, wide_r, halo_s, halo_r, leave_s, wave_r, grads_s, gin_r,
-    wout_s, wout_r, gout_s, gout_r,
+    load_s, tile_s, tile_r, level_s, level_r, wide_s, wide_r, halo_s, halo_r, leave_s, leave_r, wave_r,
+    grads_s, grads_r, gin_r, wout_s, wout_r, gout_s, gout_r,
 ):
     z, row, col = lax.axis_index("depth"), lax.axis_index("row"), lax.axis_index("col")
     ring = 2 * y_lo
@@ -124,7 +125,10 @@
     place_x = x % half
     strip = place_x * ring + y + (place_x % 2) * (ring - 1 - 2 * y)
     hub = row % 2 == 0
-    worker = hub & (z == 0)
+    home = min(HOME, depth - 1)
+    worker = hub & (z == home)
+    porter = jnp.logical_not(hub) & (z == home)
+    base_row = row - row % 2
     wide = z % RUN != 0
 
     def hub_place(tilt_index, s):
@@ -200,9 +204,13 @@
         expected += greet(wanted & jnp.logical_not(same(device)), device)
     for wanted, device in hub_tiles():
         expected += greet(wanted & jnp.logical_not(same(device)), device)
-    for plane in range(1, depth):
-        expected += greet(worker, (jnp.int32(plane), row, col))
-    expected += greet(hub & (z != 0), (jnp.int32(0), row, col))
+    for plane in range(depth):
+        if plane != home:
+            greet(worker, (jnp.int32(plane), row, col))
+    away = hub & (z != home)
+    greet(away, (jnp.int32(home), row + 1, col))
+    greet(porter, (z, base_row, col))
+    expected += (away | worker).astype(jnp.int32) + porter.astype(jnp.int32) * (depth - 1)
     expected += greet(has_left, left)
     expected += greet(has_right, right)
 
@@ -218,7 +226,7 @@
     def level_args(t):
         return intensity.at[t], levels_in.at[row], level_s.at[t], level_r, (z,) + hub_place(t, col)
 
-    @pl.when(z == 0)
+    @pl.when(z == home)
     def _():
         for t in range(2):
             push(*level_args(t))
@@ -226,56 +234,48 @@
     def turn_tiles(tiles, h):
         return jnp.concatenate([tiles[2 * h], tiles[2 * h + 1]], axis=0).T
 
-    def wide_copy():
-        return remote(wide_out, phase_w.at[z], wide_s, wide_r.at[z], (jnp.int32(0), row, col))
-
-    def own_copy():
+    def wide_args():
+        return wide_out, phase_w.at[z], wide_s, wide_r.at[z], (jnp.int32(home), row, col)
+
+    def own_args():
         span = pl.ds(32 * rim, 32 * OWN)
-        return remote(wide_out.at[span], phase_w.at[z, span], wide_s, wide_r.at[z], (jnp.int32(0), row, col))
+        return wide_out.at[span], phase_w.at[z, span], wide_s, wide_r.at[z], (jnp.int32(home), row, col)
 
     @pl.when(hub)
     def _():
         arrived(tiles_in.at[1], tile_r.at[1])
-
-        @pl.when(worker)
-        def _():
-            for h in range(2):
-                phase_w[0, 32 * rim : 32 * (rim + OWN), 128 * h : 128 * h + 128] = turn_tiles(tiles_in[1], h)
-
-        @pl.when(z != 0)
-        def _():
-            for h in range(2):
-                wide_out[32 * rim : 32 * (rim + OWN), 128 * h : 128 * h + 128] = turn_tiles(tiles_in[1], h)
-
-            @pl.when(wide)
+        for h in range(2):
+            wide_out[32 * rim : 32 * (rim + OWN), 128 * h : 128 * h + 128] = turn_tiles(tiles_in[1], h)
+
+        @pl.when(wide)
+        def _():
+            @pl.when(strip > 0)
             def _():
-                @pl.when(strip > 0)
-                def _():
-                    arrived(tiles_in.at[0], tile_r.at[0])
-                    for h in range(2):
-                        turned = turn_tiles(tiles_in[0], h)
-                        wide_out[: 32 * rim, 128 * h : 128 * h + 128] = turned[128 - 32 * rim :]
-
-                @pl.when(strip == 0)
-                def _():
-                    wide_out[: 32 * rim] = jnp.zeros((32 * rim, ROWS), F32)
-
-                @pl.when(strip < cols - 1)
-                def _():
-                    arrived(tiles_in.at[2], tile_r.at[2])
-                    for h in range(2):
-                        turned = turn_tiles(tiles_in[2], h)
-                        wide_out[32 * (rim + OWN) :, 128 * h : 128 * h + 128] = turned[: 32 * rim]
-
-                @pl.when(strip == cols - 1)
-                def _():
-                    wide_out[32 * (rim + OWN) :] = jnp.zeros((32 * rim, ROWS), F32)
-
-                wide_copy().start()
-
-            @pl.when(jnp.logical_not(wide))
+                arrived(tiles_in.at[0], tile_r.at[0])
+                for h in range(2):
+                    turned = turn_tiles(tiles_in[0], h)
+                    wide_out[: 32 * rim, 128 * h : 128 * h + 128] = turned[128 - 32 * rim :]
+
+            @pl.when(strip == 0)
             def _():
-                own_copy().start()
+                wide_out[: 32 * rim] = jnp.zeros((32 * rim, ROWS), F32)
+
+            @pl.when(strip < cols - 1)
+            def _():
+                arrived(tiles_in.at[2], tile_r.at[2])
+                for h in range(2):
+                    turned = turn_tiles(tiles_in[2], h)
+                    wide_out[32 * (rim + OWN) :, 128 * h : 128 * h + 128] = turned[: 32 * rim]
+
+            @pl.when(strip == cols - 1)
+            def _():
+                wide_out[32 * (rim + OWN) :] = jnp.zeros((32 * rim, ROWS), F32)
+
+            push(*wide_args())
+
+        @pl.when(jnp.logical_not(wide))
+        def _():
+            push(*own_args())
 
     for load in loads[2:]:
         load.wait()
@@ -345,17 +345,23 @@
     def screen_on(j, out):
         return screens[j, pl.ds(64 * (rim - out), 64 * (OWN + 2 * out))]
 
-    def leave_args(j):
-        return leaving.at[j], wave_in, leave_s.at[j], wave_r, (j, row, col)
-
-    def grads_args(j):
-        return grads.at[j], grad_in, grads_s.at[j], gin_r, (j, row, col)
+    def leave_copy(j):
+        return remote(leaving.at[j], leaving.at[j], leave_s.at[j], leave_r.at[j], (z, base_row + 1, col))
+
+    def grads_copy(j):
+        return remote(grads.at[j], grads.at[j], grads_s.at[j], grads_r.at[j], (z, base_row + 1, col))
+
+    def leave_carry(j):
+        return remote(leaving.at[j], wave_in, leave_s.at[j], wave_r, (j, base_row, col))
+
+    def grads_carry(j):
+        return remote(grads.at[j], grad_in, grads_s.at[j], gin_r, (j, base_row, col))
 
     def leave_start(j):
-        pl.when(j > 0)(remote(*leave_args(j)).start)
+        pl.when(j != home)(leave_copy(j).start)
 
     def grads_start(j):
-        pl.when(j > 0)(remote(*grads_args(j)).start)
+        pl.when(j != home)(grads_copy(j).start)
 
     def wave_turn(src):
         for c in range(2):
@@ -390,6 +396,7 @@
     def forward(k, last):
         first_slice = k * RUN
         halo_start(k)
+        pl.when(k > 0)(lambda: leave_start(first_slice - 1))
         for i in range(1, RUN + (0 if last else 1)):
             get_screen(first_slice + i, i < RUN)
         halo_wait(k)
@@ -398,8 +405,8 @@
             j = first_slice + i - 1
             wave = col_step(next_input(i, k))
             leaving[j] = own_part(wave, out)
-            leave_start(j)
             if i < RUN:
+                leave_start(j)
                 after = cmul(screen_on(j + 1, out), wave)
                 entering[j + 1] = own_part(after, out)
                 work[pl.ds(0, 64 * (OWN + 2 * out))] = row_step(after)
@@ -456,7 +463,7 @@
         incident = []
         for g in range(OWN):
             incident += [cos[32 * g : 32 * g + 32], sin[32 * g : 32 * g + 32]]
-        make_screen(0, False)
+        get_screen(0, False)
         start = cmul(screen_on(0, 0), jnp.concatenate(incident, axis=0))
         entering[0] = start
         spread[0, pl.ds(side, own_rows)] = row_step(start)
@@ -473,13 +480,32 @@
             lax.fori_loop(0, rounds - 1, forward_round, 0)
         forward(jnp.int32(rounds - 1), True)
         halo_start(rounds)
-        wave_turn(leaving.at[0])
+        leave_start(jnp.int32(slices - 1))
+        wave_turn(leaving.at[home])
         if rounds > 1:
             lax.fori_loop(rounds, 2 * rounds - 1, backward_round, 0)
         backward(jnp.int32(2 * rounds - 1), True)
-        grad_turn(grads.at[0])
-
-    @pl.when(hub & (z != 0))
+        grad_turn(grads.at[home])
+
+    @pl.when(porter)
+    def _():
+        @pl.loop(0, slices)
+        def _(j):
+            @pl.when(j != home)
+            def _():
+                leave_copy(j).wait_recv()
+                leave_carry(j).start()
+
+        @pl.loop(0, slices)
+        def _(i):
+            j = slices - 1 - i
+
+            @pl.when(j != home)
+            def _():
+                grads_copy(j).wait_recv()
+                grads_carry(j).start()
+
+    @pl.when(away)
     def _():
         arrived(wave_in, wave_r)
         wave_turn(wave_in)
@@ -497,7 +523,7 @@
             functools.partial(sent, phase.at[0], tiles_in.at[d, row], tile_s.at[t, d], tile_r.at[d], device)
         )
 
-    @pl.when(z == 0)
+    @pl.when(z == home)
     def _():
         for t in range(2):
             sent(*level_args(t))
@@ -507,8 +533,8 @@
         for r in range(4):
             sent(*wave_args(r))
             sent(*grad_args(r))
-        pl.when((z != 0) & wide)(wide_copy().wait_send)
-        pl.when((z != 0) & jnp.logical_not(wide))(own_copy().wait_send)
+        pl.when(wide)(lambda: sent(*wide_args()))
+        pl.when(jnp.logical_not(wide))(lambda: sent(*own_args()))
 
     @pl.when(worker)
     def _():
@@ -516,10 +542,14 @@
         def _(k):
             halo_sent(k)
 
-        @pl.loop(1, slices)
+    @pl.when(z == home)
+    def _():
+        @pl.loop(0, slices)
         def _(j):
-            remote(*leave_args(j)).wait_send()
-            remote(*grads_args(j)).wait_send()
+            @pl.when(j != home)
+            def _():
+                leave_copy(j).wait_send()
+                grads_copy(j).wait_send()
 
 
 def solution(mesh):
@@ -576,7 +606,9 @@
                 dma((2, rounds)),
                 dma((2, rounds)),
                 dma((slices,)),
+                dma((slices,)),
                 dma,
+                dma((slices,)),
                 dma((slices,)),
                 dma,
                 dma((4,)),
@@ -585,7 +617,7 @@
                 dma((2,)),
             ],
             compiler_params=pltpu.CompilerParams(
-                collective_id=0, has_side_effects=True, vmem_limit_bytes=56 * 2**20
+                collective_id=0, has_side_effects=True, vmem_limit_bytes=36 * 2**20
             ),
             cost_estimate=pl.CostEstimate(flops=flops, bytes_accessed=2**21, transcendentals=2**18),
         )(phase, tilt, intensity, *constants)

time: 115 us -> 113 us (0.983)
  the two profiles are of different devices: /device:TPU:67 before, /device:TPU:57 now
where the time goes in v3:
time: 113 us
  Pallas kernels  106 us (94%)
  local copies, waits for them, and re-layouts  6.34 us (6%)
    pallas_call x1, Pallas kernels, body(): pl.pallas_call(functools.partial(kernel, depth, cols, y_lo, slices), out_...  106 us
    unnamed x14, local copies, waits for them, and re-layouts  6.34 us

profile of v3, /device:TPU:57, one launch (start us, length us, event | category | flops | bytes accessed | tf_op | source)
XLA Modules:
  0.0 112.8 jit_solution(11520021996857284158)
XLA Ops:
  0.6 0.0 copy-start
  0.6 0.8 copy-done
  1.5 0.0 copy-start.1
  1.5 0.8 copy-done.1
  2.2 0.0 copy-start.2
  2.2 0.7 copy-done.2
  2.9 0.0 copy-start.3
  2.9 0.9 copy-done.3
  3.9 0.0 copy-start.4
  3.9 0.9 copy-done.4
  4.8 0.0 copy-start.5
  4.8 0.9 copy-done.5
  5.7 105.8 %shard_map.77 = (f32[1,64,128]{2,1,0:T(8,128)S(1)}, f32[2,1,2,64,128]{4,3,2,1,0:T(8,128)S(1)}) custom-call(f32[1,64,128]{2,1,0:T(8,128)S(1)} %copy-done.1, s32[2,2]{1,0:T(2,128)S(1)} %copy-done.2, f32[2,64,128]{2,1,0:T(8,128)S(1)} %copy-done, bf16[256,512]{1,0:T(8,128)(2,1)S(1)} %copy-done.4, bf16[256,512]{1,0:T(8,128)(2,1)S(1)} %copy-done.3, ...), custom_call_target="tpu_custom_call" | custom-call | flops 12683575296 | bytes 2097152 | tf_op jit(solution)/shard_map/pallas_call | solution.py:569
  111.5 0.6 copy.10
  112.2 0.7 copy.11
Async XLA Ops:
  0.6 0.8 copy-start
  1.5 0.8 copy-start.1
  2.2 0.7 copy-start.2
  2.9 0.9 copy-start.3
  3.9 0.9 copy-start.4
  4.8 0.9 copy-start.5

commit v4 on v3

--- a/solution.py
+++ b/solution.py
@@ -94,9 +94,9 @@
     phase_h, tilt_h, intensity_h, row_high_h, row_low_h, pair_h,
     grad, waves,
     phase, tilt, intensity, row_high, row_low, pair,
-    tiles_in, levels_in, wide_out, phase_w, screens, entering, leaving, spread, work, grads,
+    tiles_in, levels_in, strip_out, phase_w, screens, entering, leaving, spread, work, grads,
     wave_in, grad_in, wave_out, grad_out, grad_tiles,
-    load_s, tile_s, tile_r, level_s, level_r, wide_s, wide_r, halo_s, halo_r, leave_s, leave_r, wave_r,
+    load_s, tile_s, tile_r, level_s, level_r, strip_s, strip_r, halo_s, halo_r, leave_s, leave_r, wave_r,
     grads_s, grads_r, gin_r, wout_s, wout_r, gout_s, gout_r,
 ):
     z, row, col = lax.axis_index("depth"), lax.axis_index("row"), lax.axis_index("col")
@@ -172,23 +172,27 @@
     def arrived(buffer, recv):
         pltpu.make_async_copy(buffer, buffer, recv).wait()
 
-    def tile_hubs():
-        for t in range(2):
-            for d in range(3):
-                s = col + 1 - d
-                wanted = (s >= 0) & (s < cols)
-                if d != 1:
-                    wanted = wanted & wide
-                yield t, d, wanted, (z,) + hub_place(t, clamp(s))
-
-    def hub_tiles():
-        for d in range(3):
-            c = strip + d - 1
-            wanted = hub & (c >= 0) & (c < cols)
-            if d != 1:
-                wanted = wanted & wide
-            for r in range(4):
-                yield wanted, (z, jnp.int32(r), clamp(c))
+    def tile_args(t):
+        return phase.at[0], tiles_in.at[row], tile_s.at[t], tile_r, (z,) + hub_place(t, col)
+
+    def strip_args(side_of):
+        s = strip + side_of
+        device = (jnp.int32(home),) + hub_place(b, clamp(s))
+        if side_of == 0:
+            src, at, size = 0, 32 * rim, 32 * OWN
+        elif side_of < 0:
+            src, at, size = 0, 32 * (rim + OWN), 32 * rim
+        else:
+            src, at, size = 32 * (OWN - rim), 0, 32 * rim
+        return (
+            strip_out.at[pl.ds(src, size)], phase_w.at[z, pl.ds(at, size)],
+            strip_s.at[side_of + 1], strip_r.at[1 - side_of, z], device,
+        )
+
+    def strip_wanted(side_of):
+        if side_of == 0:
+            return hub
+        return hub & wide & (strip + side_of >= 0) & (strip + side_of < cols)
 
     barrier = pltpu.get_barrier_semaphore()
 
@@ -200,17 +204,26 @@
         return condition.astype(jnp.int32)
 
     expected = jnp.int32(0)
-    for _, _, wanted, device in tile_hubs():
-        expected += greet(wanted & jnp.logical_not(same(device)), device)
-    for wanted, device in hub_tiles():
-        expected += greet(wanted & jnp.logical_not(same(device)), device)
+    for t in range(2):
+        device = (z,) + hub_place(t, col)
+        expected += greet(jnp.logical_not(same(device)), device)
+    for r in range(4):
+        device = (z, jnp.int32(r), strip)
+        expected += greet(hub & jnp.logical_not(same(device)), device)
+    away = hub & (z != home)
     for plane in range(depth):
         if plane != home:
             greet(worker, (jnp.int32(plane), row, col))
-    away = hub & (z != home)
+            if plane % RUN != 0:
+                greet(has_left, (jnp.int32(plane),) + left[1:])
+                greet(has_right, (jnp.int32(plane),) + right[1:])
+    for side_of in (-1, 0, 1):
+        expected += (strip_wanted(side_of) & (z != home)).astype(jnp.int32)
     greet(away, (jnp.int32(home), row + 1, col))
     greet(porter, (z, base_row, col))
-    expected += (away | worker).astype(jnp.int32) + porter.astype(jnp.int32) * (depth - 1)
+    early = away & (z < home)
+    greet(early, (jnp.int32(home), row, col))
+    expected += worker.astype(jnp.int32) * (1 + home) + porter.astype(jnp.int32) * (depth - 1)
     expected += greet(has_left, left)
     expected += greet(has_right, right)
 
@@ -218,10 +231,8 @@
     loads[1].wait()
     pl.semaphore_wait(barrier, expected)
 
-    for t, d, wanted, device in tile_hubs():
-        pl.when(wanted)(
-            functools.partial(push, phase.at[0], tiles_in.at[d, row], tile_s.at[t, d], tile_r.at[d], device)
-        )
+    for t in range(2):
+        push(*tile_args(t))
 
     def level_args(t):
         return intensity.at[t], levels_in.at[row], level_s.at[t], level_r, (z,) + hub_place(t, col)
@@ -234,48 +245,13 @@
     def turn_tiles(tiles, h):
         return jnp.concatenate([tiles[2 * h], tiles[2 * h + 1]], axis=0).T
 
-    def wide_args():
-        return wide_out, phase_w.at[z], wide_s, wide_r.at[z], (jnp.int32(home), row, col)
-
-    def own_args():
-        span = pl.ds(32 * rim, 32 * OWN)
-        return wide_out.at[span], phase_w.at[z, span], wide_s, wide_r.at[z], (jnp.int32(home), row, col)
-
     @pl.when(hub)
     def _():
-        arrived(tiles_in.at[1], tile_r.at[1])
+        arrived(tiles_in, tile_r)
         for h in range(2):
-            wide_out[32 * rim : 32 * (rim + OWN), 128 * h : 128 * h + 128] = turn_tiles(tiles_in[1], h)
-
-        @pl.when(wide)
-        def _():
-            @pl.when(strip > 0)
-            def _():
-                arrived(tiles_in.at[0], tile_r.at[0])
-                for h in range(2):
-                    turned = turn_tiles(tiles_in[0], h)
-                    wide_out[: 32 * rim, 128 * h : 128 * h + 128] = turned[128 - 32 * rim :]
-
-            @pl.when(strip == 0)
-            def _():
-                wide_out[: 32 * rim] = jnp.zeros((32 * rim, ROWS), F32)
-
-            @pl.when(strip < cols - 1)
-            def _():
-                arrived(tiles_in.at[2], tile_r.at[2])
-                for h in range(2):
-                    turned = turn_tiles(tiles_in[2], h)
-                    wide_out[32 * (rim + OWN) :, 128 * h : 128 * h + 128] = turned[: 32 * rim]
-
-            @pl.when(strip == cols - 1)
-            def _():
-                wide_out[32 * (rim + OWN) :] = jnp.zeros((32 * rim, ROWS), F32)
-
-            push(*wide_args())
-
-        @pl.when(jnp.logical_not(wide))
-        def _():
-            push(*own_args())
+            strip_out[:, 128 * h : 128 * h + 128] = turn_tiles(tiles_in, h)
+        for side_of in (0, -1, 1):
+            pl.when(strip_wanted(side_of))(functools.partial(push, *strip_args(side_of)))
 
     for load in loads[2:]:
         load.wait()
@@ -335,11 +311,12 @@
             screens[j, 64 * g + 32 : 64 * g + 64] = s
 
     def get_screen(j, with_rim):
+        span = pl.ds(32 * rim, 32 * OWN)
+        arrived(phase_w.at[j, span], strip_r.at[1, j])
         if with_rim:
-            arrived(phase_w.at[j], wide_r.at[j])
-        else:
-            span = pl.ds(32 * rim, 32 * OWN)
-            arrived(phase_w.at[j, span], wide_r.at[j])
+            low, high = pl.ds(0, 32 * rim), pl.ds(32 * (rim + OWN), 32 * rim)
+            pl.when(strip > 0)(lambda: arrived(phase_w.at[j, low], strip_r.at[0, j]))
+            pl.when(strip < cols - 1)(lambda: arrived(phase_w.at[j, high], strip_r.at[2, j]))
         make_screen(j, with_rim)
 
     def screen_on(j, out):
@@ -361,7 +338,8 @@
         pl.when(j != home)(leave_copy(j).start)
 
     def grads_start(j):
-        pl.when(j != home)(grads_copy(j).start)
+        pl.when(j > home)(grads_copy(j).start)
+        pl.when(j < home)(grads_carry(j).start)
 
     def wave_turn(src):
         for c in range(2):
@@ -397,8 +375,8 @@
         first_slice = k * RUN
         halo_start(k)
         pl.when(k > 0)(lambda: leave_start(first_slice - 1))
-        for i in range(1, RUN + (0 if last else 1)):
-            get_screen(first_slice + i, i < RUN)
+        for i in range(1, RUN):
+            get_screen(first_slice + i, True)
         halo_wait(k)
         for i in range(1, RUN + 1):
             out = RUN - i
@@ -407,6 +385,9 @@
             leaving[j] = own_part(wave, out)
             if i < RUN:
                 leave_start(j)
+            elif not last:
+                get_screen(j + 1, False)
+            if i < RUN:
                 after = cmul(screen_on(j + 1, out), wave)
                 entering[j + 1] = own_part(after, out)
                 work[pl.ds(0, 64 * (OWN + 2 * out))] = row_step(after)
@@ -449,11 +430,19 @@
             def _(k):
                 spread[k, pl.ds(0, side)] = jnp.zeros((side, ROWS), F32)
 
+            @pl.loop(0, slices)
+            def _(j):
+                phase_w[j, pl.ds(0, 32 * rim)] = jnp.zeros((32 * rim, ROWS), F32)
+
         @pl.when(strip == cols - 1)
         def _():
             @pl.loop(0, 2 * rounds)
             def _(k):
                 spread[k, pl.ds(side + own_rows, side)] = jnp.zeros((side, ROWS), F32)
+
+            @pl.loop(0, slices)
+            def _(j):
+                phase_w[j, pl.ds(32 * (rim + OWN), 32 * rim)] = jnp.zeros((32 * rim, ROWS), F32)
 
         row_pos = lax.broadcasted_iota(jnp.int32, (32 * OWN, ROWS), 1).astype(F32)
         col_pos = (strip * (32 * OWN) + lax.broadcasted_iota(jnp.int32, (32 * OWN, ROWS), 0)).astype(F32)
@@ -500,7 +489,7 @@
         def _(i):
             j = slices - 1 - i
 
-            @pl.when(j != home)
+            @pl.when(j > home)
             def _():
                 grads_copy(j).wait_recv()
                 grads_carry(j).start()
@@ -518,10 +507,8 @@
         arrived(grad_tiles.at[t], gout_r.at[t])
     grad[0] = grad_tiles[0] + grad_tiles[1]
 
-    for t, d, wanted, device in tile_hubs():
-        pl.when(wanted)(
-            functools.partial(sent, phase.at[0], tiles_in.at[d, row], tile_s.at[t, d], tile_r.at[d], device)
-        )
+    for t in range(2):
+        sent(*tile_args(t))
 
     @pl.when(z == home)
     def _():
@@ -533,8 +520,8 @@
         for r in range(4):
             sent(*wave_args(r))
             sent(*grad_args(r))
-        pl.when(wide)(lambda: sent(*wide_args()))
-        pl.when(jnp.logical_not(wide))(lambda: sent(*own_args()))
+        for side_of in (-1, 0, 1):
+            pl.when(strip_wanted(side_of))(functools.partial(sent, *strip_args(side_of)))
 
     @pl.when(worker)
     def _():
@@ -549,7 +536,7 @@
             @pl.when(j != home)
             def _():
                 leave_copy(j).wait_send()
-                grads_copy(j).wait_send()
+                pl.when(hub | (j > home))(grads_copy(j).wait_send)
 
 
 def solution(mesh):
@@ -581,9 +568,9 @@
                 pltpu.VMEM((ROWS, 2 * ROWS), BF16),
                 pltpu.VMEM((ROWS, 2 * ROWS), BF16),
                 pltpu.VMEM((256, 256), BF16),
-                pltpu.VMEM((3, 4, 64, 128), F32),
                 pltpu.VMEM((4, 64, 128), F32),
-                pltpu.VMEM((32 * reach, ROWS), F32),
+                pltpu.VMEM((4, 64, 128), F32),
+                pltpu.VMEM((32 * OWN, ROWS), F32),
                 pltpu.VMEM((slices, 32 * reach, ROWS), F32),
                 pltpu.VMEM((slices, 64 * reach, ROWS), F32),
                 pltpu.VMEM((slices,) + strip, F32),
@@ -597,12 +584,12 @@
                 pltpu.VMEM((4, 64, 128), F32),
                 pltpu.VMEM((2, 64, 128), F32),
                 dma((6,)),
-                dma((2, 3)),
-                dma((3,)),
                 dma((2,)),
                 dma,
+                dma((2,)),
                 dma,
-                dma((slices,)),
+                dma((3,)),
+                dma((3, slices)),
                 dma((2, rounds)),
                 dma((2, rounds)),
                 dma((slices,)),
@@ -617,7 +604,7 @@
                 dma((2,)),
             ],
             compiler_params=pltpu.CompilerParams(
-                collective_id=0, has_side_effects=True, vmem_limit_bytes=36 * 2**20
+                collective_id=0, has_side_effects=True, vmem_limit_bytes=56 * 2**20
             ),
             cost_estimate=pl.CostEstimate(flops=flops, bytes_accessed=2**21, transcendentals=2**18),
         )(phase, tilt, intensity, *constants)

time: 113 us -> 115 us (1.018)
  Pallas kernels: 106 us -> 111 us
  local copies, waits for them, and re-layouts: 6.34 us -> 2.94 us
    pallas_call x1, Pallas kernels: 106 us -> 111 us  [body(): pl.pallas_call(functools.partial(kernel, depth, cols, y_lo, slices), out_...]
    unnamed x14 -> x2, local copies, waits for them, and re-layouts: 6.34 us -> 2.94 us
where the time goes in v4:
time: 115 us
  Pallas kernels  111 us (97%)
  local copies, waits for them, and re-layouts  2.94 us (3%)
    pallas_call x1, Pallas kernels, body(): pl.pallas_call(functools.partial(kernel, depth, cols, y_lo, slices), out_...  111 us
    unnamed x2, local copies, waits for them, and re-layouts  2.94 us

profile of v4, /device:TPU:57, one launch (start us, length us, event | category | flops | bytes accessed | tf_op | source)
XLA Modules:
  0.0 114.9 jit_solution(14356584289746668779)
XLA Ops:
  0.6 111.3 %shard_map.77 = (f32[1,64,128]{2,1,0:T(8,128)}, f32[2,1,2,64,128]{4,3,2,1,0:T(8,128)}) custom-call(f32[1,64,128]{2,1,0:T(8,128)} %phase_h.1, s32[2,2]{1,0:T(2,128)} %tilt_h.1, f32[2,64,128]{2,1,0:T(8,128)} %intensity_h.1, bf16[256,512]{1,0:T(8,128)(2,1)} %constant.6.clone.row_high_h, bf16[256,512]{1,0:T(8,128)(2,1)} %constant.7.clone.row_low_h, ...), custom_call_target="tpu_custom_call" | custom-call | flops 12683575296 | bytes 2097152 | tf_op jit(solution)/shard_map/pallas_call | solution.py:556
  111.9 1.4 %copy.10 = f32[1,64,128]{2,1,0:T(8,128)} copy(f32[1,64,128]{2,1,0:T(8,128)} %get-tuple-element.4) | data formatting | bytes 65536
  113.3 1.6 %copy.11 = f32[2,1,2,64,128]{4,3,2,1,0:T(8,128)} copy(f32[2,1,2,64,128]{4,3,2,1,0:T(8,128)} %get-tuple-element.5) | data formatting | bytes 262144

commit v5 on v4

--- a/solution.py
+++ b/solution.py
@@ -15,7 +15,7 @@
 OWN = 4
 RUN = 4
 ROWS = 256
-HOME = 2
+HOME = 1
 MESH = pl.DeviceIdType.MESH
 F32 = jnp.float32
 BF16 = jnp.bfloat16
@@ -97,7 +97,7 @@
     tiles_in, levels_in, strip_out, phase_w, screens, entering, leaving, spread, work, grads,
     wave_in, grad_in, wave_out, grad_out, grad_tiles,
     load_s, tile_s, tile_r, level_s, level_r, strip_s, strip_r, halo_s, halo_r, leave_s, leave_r, wave_r,
-    grads_s, grads_r, gin_r, wout_s, wout_r, gout_s, gout_r,
+    grads_s, grads_r, gin_r, wout_s, wout_r, gout_s, gout_r, ready,
 ):
     z, row, col = lax.axis_index("depth"), lax.axis_index("row"), lax.axis_index("col")
     ring = 2 * y_lo
@@ -217,13 +217,14 @@
             if plane % RUN != 0:
                 greet(has_left, (jnp.int32(plane),) + left[1:])
                 greet(has_right, (jnp.int32(plane),) + right[1:])
+            for r in range(4 if plane < home else 0):
+                greet(worker, (jnp.int32(plane), jnp.int32(r), strip))
+            greet(porter, (jnp.int32(plane), base_row, col))
     for side_of in (-1, 0, 1):
         expected += (strip_wanted(side_of) & (z != home)).astype(jnp.int32)
-    greet(away, (jnp.int32(home), row + 1, col))
     greet(porter, (z, base_row, col))
-    early = away & (z < home)
-    greet(early, (jnp.int32(home), row, col))
-    expected += worker.astype(jnp.int32) * (1 + home) + porter.astype(jnp.int32) * (depth - 1)
+    early = z < home
+    expected += away.astype(jnp.int32) + worker.astype(jnp.int32) + 2 * early.astype(jnp.int32)
     expected += greet(has_left, left)
     expected += greet(has_right, right)
 
@@ -231,8 +232,18 @@
     loads[1].wait()
     pl.semaphore_wait(barrier, expected)
 
+    def ready_signal(condition, device):
+        @pl.when(condition)
+        def _():
+            pl.semaphore_signal(ready, inc=1, device_id=device, device_id_type=MESH)
+
+
     for t in range(2):
         push(*tile_args(t))
+
+    ready_signal(away, (jnp.int32(home), row + 1, col))
+    for t in range(2):
+        ready_signal(early, (jnp.int32(home),) + hub_place(t, col))
 
     def level_args(t):
         return intensity.at[t], levels_in.at[row], level_s.at[t], level_r, (z,) + hub_place(t, col)
@@ -339,7 +350,6 @@
 
     def grads_start(j):
         pl.when(j > home)(grads_copy(j).start)
-        pl.when(j < home)(grads_carry(j).start)
 
     def wave_turn(src):
         for c in range(2):
@@ -354,16 +364,17 @@
     def wave_args(r):
         return wave_out.at[r], waves.at[b, 0], wout_s.at[r], wout_r.at[b], (z, jnp.int32(r), strip)
 
-    def grad_turn(src):
+    def grad_turn(src, plane, slot):
         for h in range(2):
             turned = src[:, 128 * h : 128 * h + 128].T
-            grad_out[2 * h] = turned[:64]
-            grad_out[2 * h + 1] = turned[64:]
+            grad_out[slot, 2 * h] = turned[:64]
+            grad_out[slot, 2 * h + 1] = turned[64:]
         for r in range(4):
-            push(*grad_args(r))
-
-    def grad_args(r):
-        return grad_out.at[r], grad_tiles.at[b], gout_s.at[r], gout_r.at[b], (z, jnp.int32(r), strip)
+            push(*grad_args(r, plane, slot))
+
+    def grad_args(r, plane, slot):
+        device = (plane, jnp.int32(r), strip)
+        return grad_out.at[slot, r], grad_tiles.at[b], gout_s.at[slot, r], gout_r.at[b], device
 
     def next_input(i, k):
         return spread[k] if i == 1 else work[pl.ds(0, 64 * (OWN + 2 * (RUN - i + 1)))]
@@ -420,7 +431,13 @@
             for (pr, pi), (er, ei) in zip(blocks_of(own_part(pulled, out)), blocks_of(entering[j])):
                 parts.append(-(pr * ei + pi * er))
             grads[j] = jnp.concatenate(parts, axis=0)
-            grads_start(j)
+            if last and RUN - i <= home:
+                plane = RUN - i
+                if plane == home - 1:
+                    pl.semaphore_wait(ready, 4 * home)
+                grad_turn(grads.at[plane], jnp.int32(plane), plane)
+            else:
+                grads_start(j)
 
     @pl.when(worker)
     def _():
@@ -474,10 +491,11 @@
         if rounds > 1:
             lax.fori_loop(rounds, 2 * rounds - 1, backward_round, 0)
         backward(jnp.int32(2 * rounds - 1), True)
-        grad_turn(grads.at[home])
 
     @pl.when(porter)
     def _():
+        pl.semaphore_wait(ready, depth - 1)
+
         @pl.loop(0, slices)
         def _(j):
             @pl.when(j != home)
@@ -498,8 +516,11 @@
     def _():
         arrived(wave_in, wave_r)
         wave_turn(wave_in)
-        arrived(grad_in, gin_r)
-        grad_turn(grad_in)
+
+        @pl.when(z > home)
+        def _():
+            arrived(grad_in, gin_r)
+            grad_turn(grad_in, z, 0)
 
     for t in range(2):
         arrived(waves.at[t, 0], wout_r.at[t])
@@ -519,7 +540,9 @@
     def _():
         for r in range(4):
             sent(*wave_args(r))
-            sent(*grad_args(r))
+            for plane in range(home + 1):
+                pl.when(worker)(functools.partial(sent, *grad_args(r, jnp.int32(plane), plane)))
+            pl.when(z > home)(functools.partial(sent, *grad_args(r, z, 0)))
         for side_of in (-1, 0, 1):
             pl.when(strip_wanted(side_of))(functools.partial(sent, *strip_args(side_of)))
 
@@ -536,7 +559,7 @@
             @pl.when(j != home)
             def _():
                 leave_copy(j).wait_send()
-                pl.when(hub | (j > home))(grads_copy(j).wait_send)
+                pl.when(j > home)(grads_copy(j).wait_send)
 
 
 def solution(mesh):
@@ -581,7 +604,7 @@
                 pltpu.VMEM(strip, F32),
                 pltpu.VMEM((32 * OWN, ROWS), F32),
                 pltpu.VMEM((4, 2, 64, 128), F32),
-                pltpu.VMEM((4, 64, 128), F32),
+                pltpu.VMEM((HOME + 1, 4, 64, 128), F32),
                 pltpu.VMEM((2, 64, 128), F32),
                 dma((6,)),
                 dma((2,)),
@@ -600,8 +623,9 @@
                 dma,
                 dma((4,)),
                 dma((2,)),
-                dma((4,)),
+                dma((HOME + 1, 4)),
                 dma((2,)),
+                pltpu.SemaphoreType.REGULAR,
             ],
             compiler_params=pltpu.CompilerParams(
                 collective_id=0, has_side_effects=True, vmem_limit_bytes=56 * 2**20

time: 115 us -> 114 us (level)
  no operation moved by 1% of the time
where the time goes in v5:
time: 114 us
  Pallas kernels  111 us (97%)
  local copies, waits for them, and re-layouts  2.94 us (3%)
    pallas_call x1, Pallas kernels, body(): pl.pallas_call(functools.partial(kernel, depth, cols, y_lo, slices), out_...  111 us
    unnamed x2, local copies, waits for them, and re-layouts  2.94 us

profile of v5, /device:TPU:57, one launch (start us, length us, event | category | flops | bytes accessed | tf_op | source)
XLA Modules:
  0.0 114.1 jit_solution(4178770827358707520)
XLA Ops:
  0.6 110.5 %shard_map.77 = (f32[1,64,128]{2,1,0:T(8,128)}, f32[2,1,2,64,128]{4,3,2,1,0:T(8,128)}) custom-call(f32[1,64,128]{2,1,0:T(8,128)} %phase_h.1, s32[2,2]{1,0:T(2,128)} %tilt_h.1, f32[2,64,128]{2,1,0:T(8,128)} %intensity_h.1, bf16[256,512]{1,0:T(8,128)(2,1)} %constant.6.clone.row_high_h, bf16[256,512]{1,0:T(8,128)(2,1)} %constant.7.clone.row_low_h, ...), custom_call_target="tpu_custom_call" | custom-call | flops 12683575296 | bytes 2097152 | tf_op jit(solution)/shard_map/pallas_call | solution.py:579
  111.1 1.4 %copy.10 = f32[1,64,128]{2,1,0:T(8,128)} copy(f32[1,64,128]{2,1,0:T(8,128)} %get-tuple-element.4) | data formatting | bytes 65536
  112.5 1.6 %copy.11 = f32[2,1,2,64,128]{4,3,2,1,0:T(8,128)} copy(f32[2,1,2,64,128]{4,3,2,1,0:T(8,128)} %get-tuple-element.5) | data formatting | bytes 262144

commit v6 on v3

--- a/solution.py
+++ b/solution.py
@@ -97,7 +97,7 @@
     tiles_in, levels_in, wide_out, phase_w, screens, entering, leaving, spread, work, grads,
     wave_in, grad_in, wave_out, grad_out, grad_tiles,
     load_s, tile_s, tile_r, level_s, level_r, wide_s, wide_r, halo_s, halo_r, leave_s, leave_r, wave_r,
-    grads_s, grads_r, gin_r, wout_s, wout_r, gout_s, gout_r,
+    grads_s, grads_r, gin_r, wout_s, wout_r, gout_s, gout_r, ready,
 ):
     z, row, col = lax.axis_index("depth"), lax.axis_index("row"), lax.axis_index("col")
     ring = 2 * y_lo
@@ -204,24 +204,38 @@
         expected += greet(wanted & jnp.logical_not(same(device)), device)
     for wanted, device in hub_tiles():
         expected += greet(wanted & jnp.logical_not(same(device)), device)
+    away = hub & (z != home)
     for plane in range(depth):
         if plane != home:
             greet(worker, (jnp.int32(plane), row, col))
-    away = hub & (z != home)
-    greet(away, (jnp.int32(home), row + 1, col))
+            for r in range(4 if plane < home else 0):
+                greet(worker, (jnp.int32(plane), jnp.int32(r), strip))
+            greet(porter, (jnp.int32(plane), base_row, col))
+    expected += away.astype(jnp.int32)
     greet(porter, (z, base_row, col))
-    expected += (away | worker).astype(jnp.int32) + porter.astype(jnp.int32) * (depth - 1)
+    early = z < home
+    expected += away.astype(jnp.int32) + worker.astype(jnp.int32) + 2 * early.astype(jnp.int32)
     expected += greet(has_left, left)
     expected += greet(has_right, right)
 
     loads[0].wait()
     loads[1].wait()
     pl.semaphore_wait(barrier, expected)
+
+    def ready_signal(condition, device):
+        @pl.when(condition)
+        def _():
+            pl.semaphore_signal(ready, inc=1, device_id=device, device_id_type=MESH)
+
 
     for t, d, wanted, device in tile_hubs():
         pl.when(wanted)(
             functools.partial(push, phase.at[0], tiles_in.at[d, row], tile_s.at[t, d], tile_r.at[d], device)
         )
+
+    ready_signal(away, (jnp.int32(home), row + 1, col))
+    for t in range(2):
+        ready_signal(early, (jnp.int32(home),) + hub_place(t, col))
 
     def level_args(t):
         return intensity.at[t], levels_in.at[row], level_s.at[t], level_r, (z,) + hub_place(t, col)
@@ -298,31 +312,31 @@
         return jnp.concatenate(out, axis=0)
 
     def halo_copies(k):
-        return (
+        part = side // 2
+        far_right = side + own_rows
+        spans = (
+            (side, far_right, left), (own_rows + part, part, right),
+            (side + part, far_right + part, left), (own_rows, 0, right),
+        )
+        return [
             remote(
-                spread.at[k, pl.ds(side, side)], spread.at[k, pl.ds(side + own_rows, side)],
-                halo_s.at[0, k], halo_r.at[1, k], left,
-            ),
-            remote(
-                spread.at[k, pl.ds(own_rows, side)], spread.at[k, pl.ds(0, side)],
-                halo_s.at[1, k], halo_r.at[0, k], right,
-            ),
-        )
+                spread.at[k, pl.ds(src, part)], spread.at[k, pl.ds(dst, part)], halo_s.at[n, k], halo_r.at[n, k], device
+            )
+            for n, (src, dst, device) in enumerate(spans)
+        ]
 
     def halo_start(k):
-        to_left, to_right = halo_copies(k)
-        pl.when(has_left)(to_left.start)
-        pl.when(has_right)(to_right.start)
-
-    def halo_wait(k):
-        to_left, to_right = halo_copies(k)
-        pl.when(has_left)(to_right.wait_recv)
-        pl.when(has_right)(to_left.wait_recv)
+        for n, copy in enumerate(halo_copies(k)):
+            pl.when(has_right if n % 2 else has_left)(copy.start)
+
+    def halo_wait(k, far):
+        copies = halo_copies(k)[2 * far : 2 * far + 2]
+        pl.when(has_right)(copies[0].wait_recv)
+        pl.when(has_left)(copies[1].wait_recv)
 
     def halo_sent(k):
-        to_left, to_right = halo_copies(k)
-        pl.when(has_left)(to_left.wait_send)
-        pl.when(has_right)(to_right.wait_send)
+        for n, copy in enumerate(halo_copies(k)):
+            pl.when(has_right if n % 2 else has_left)(copy.wait_send)
 
     def make_screen(j, with_rim):
         for g in range(0 if with_rim else rim, OWN + (2 * rim if with_rim else rim)):
@@ -361,7 +375,7 @@
         pl.when(j != home)(leave_copy(j).start)
 
     def grads_start(j):
-        pl.when(j != home)(grads_copy(j).start)
+        pl.when(j > home)(grads_copy(j).start)
 
     def wave_turn(src):
         for c in range(2):
@@ -376,19 +390,39 @@
     def wave_args(r):
         return wave_out.at[r], waves.at[b, 0], wout_s.at[r], wout_r.at[b], (z, jnp.int32(r), strip)
 
-    def grad_turn(src):
+    def grad_turn(src, plane, slot):
         for h in range(2):
             turned = src[:, 128 * h : 128 * h + 128].T
-            grad_out[2 * h] = turned[:64]
-            grad_out[2 * h + 1] = turned[64:]
+            grad_out[slot, 2 * h] = turned[:64]
+            grad_out[slot, 2 * h + 1] = turned[64:]
         for r in range(4):
-            push(*grad_args(r))
-
-    def grad_args(r):
-        return grad_out.at[r], grad_tiles.at[b], gout_s.at[r], gout_r.at[b], (z, jnp.int32(r), strip)
-
-    def next_input(i, k):
-        return spread[k] if i == 1 else work[pl.ds(0, 64 * (OWN + 2 * (RUN - i + 1)))]
+            push(*grad_args(r, plane, slot))
+
+    def grad_args(r, plane, slot):
+        device = (plane, jnp.int32(r), strip)
+        return grad_out.at[slot, r], grad_tiles.at[b], gout_s.at[slot, r], gout_r.at[b], device
+
+    def next_input(i):
+        return work[pl.ds(0, 64 * (OWN + 2 * (RUN - i + 1)))]
+
+    def first_pairs(k, j, pairs, adjoint):
+        wave = jnp.concatenate([col_step(spread[k, pl.ds(128 * p, 256)]) for p in pairs], axis=0)
+        screen = jnp.concatenate([screens[j if adjoint else j + 1, pl.ds(128 * p, 128)] for p in pairs], axis=0)
+        after = cmul(screen, wave)
+        onward = row_step(after)
+        for n, p in enumerate(pairs):
+            work[pl.ds(128 * p, 128)] = onward[128 * n : 128 * n + 128]
+            for o in range(2):
+                own = 2 * p + o - rim
+                if 0 <= own < OWN:
+                    at = 128 * n + 64 * o
+                    if adjoint:
+                        entered = entering[j, pl.ds(64 * own, 64)]
+                        pr, pi = wave[at : at + 32], wave[at + 32 : at + 64]
+                        grads[j, pl.ds(32 * own, 32)] = -(pr * entered[32:] + pi * entered[:32])
+                    else:
+                        leaving[j, pl.ds(64 * own, 64)] = wave[at : at + 64]
+                        entering[j + 1, pl.ds(64 * own, 64)] = after[at : at + 64]
 
     def own_part(value, out):
         return value[64 * out : 64 * out + own_rows]
@@ -397,16 +431,25 @@
         first_slice = k * RUN
         halo_start(k)
         pl.when(k > 0)(lambda: leave_start(first_slice - 1))
-        for i in range(1, RUN + (0 if last else 1)):
-            get_screen(first_slice + i, i < RUN)
-        halo_wait(k)
-        for i in range(1, RUN + 1):
+        get_screen(first_slice + 1, True)
+        first_pairs(k, first_slice, [2], False)
+        for i in range(2, RUN):
+            get_screen(first_slice + i, True)
+        halo_wait(k, 0)
+        first_pairs(k, first_slice, [1, 3], False)
+        halo_wait(k, 1)
+        first_pairs(k, first_slice, [0, 4], False)
+        leave_start(first_slice)
+        for i in range(2, RUN + 1):
             out = RUN - i
             j = first_slice + i - 1
-            wave = col_step(next_input(i, k))
+            wave = col_step(next_input(i))
             leaving[j] = own_part(wave, out)
             if i < RUN:
                 leave_start(j)
+            elif not last:
+                get_screen(j + 1, False)
+            if i < RUN:
                 after = cmul(screen_on(j + 1, out), wave)
                 entering[j + 1] = own_part(after, out)
                 work[pl.ds(0, 64 * (OWN + 2 * out))] = row_step(after)
@@ -425,11 +468,16 @@
 
     def backward(k, last):
         first_slice = (2 * rounds - k) * RUN - 1
-        halo_wait(k)
-        for i in range(1, RUN + 1):
+        first_pairs(k, first_slice, [2], True)
+        halo_wait(k, 0)
+        first_pairs(k, first_slice, [1, 3], True)
+        halo_wait(k, 1)
+        first_pairs(k, first_slice, [0, 4], True)
+        grads_start(first_slice)
+        for i in range(2, RUN + 1):
             out = RUN - i
             j = first_slice - (i - 1)
-            pulled = col_step(next_input(i, k))
+            pulled = col_step(next_input(i))
             if i < RUN:
                 work[pl.ds(0, 64 * (OWN + 2 * out))] = row_step(cmul(screen_on(j, out), pulled))
             elif not last:
@@ -439,7 +487,13 @@
             for (pr, pi), (er, ei) in zip(blocks_of(own_part(pulled, out)), blocks_of(entering[j])):
                 parts.append(-(pr * ei + pi * er))
             grads[j] = jnp.concatenate(parts, axis=0)
-            grads_start(j)
+            if last and RUN - i <= home:
+                plane = RUN - i
+                if plane == home - 1:
+                    pl.semaphore_wait(ready, 4 * home)
+                grad_turn(grads.at[plane], jnp.int32(plane), plane)
+            else:
+                grads_start(j)
 
     @pl.when(worker)
     def _():
@@ -485,10 +539,11 @@
         if rounds > 1:
             lax.fori_loop(rounds, 2 * rounds - 1, backward_round, 0)
         backward(jnp.int32(2 * rounds - 1), True)
-        grad_turn(grads.at[home])
 
     @pl.when(porter)
     def _():
+        pl.semaphore_wait(ready, depth - 1)
+
         @pl.loop(0, slices)
         def _(j):
             @pl.when(j != home)
@@ -500,7 +555,7 @@
         def _(i):
             j = slices - 1 - i
 
-            @pl.when(j != home)
+            @pl.when(j > home)
             def _():
                 grads_copy(j).wait_recv()
                 grads_carry(j).start()
@@ -509,8 +564,11 @@
     def _():
         arrived(wave_in, wave_r)
         wave_turn(wave_in)
-        arrived(grad_in, gin_r)
-        grad_turn(grad_in)
+
+        @pl.when(z > home)
+        def _():
+            arrived(grad_in, gin_r)
+            grad_turn(grad_in, z, 0)
 
     for t in range(2):
         arrived(waves.at[t, 0], wout_r.at[t])
@@ -532,7 +590,9 @@
     def _():
         for r in range(4):
             sent(*wave_args(r))
-            sent(*grad_args(r))
+            for plane in range(home + 1):
+                pl.when(worker)(functools.partial(sent, *grad_args(r, jnp.int32(plane), plane)))
+            pl.when(z > home)(functools.partial(sent, *grad_args(r, z, 0)))
         pl.when(wide)(lambda: sent(*wide_args()))
         pl.when(jnp.logical_not(wide))(lambda: sent(*own_args()))
 
@@ -549,7 +609,7 @@
             @pl.when(j != home)
             def _():
                 leave_copy(j).wait_send()
-                grads_copy(j).wait_send()
+                pl.when(j > home)(grads_copy(j).wait_send)
 
 
 def solution(mesh):
@@ -594,7 +654,7 @@
                 pltpu.VMEM(strip, F32),
                 pltpu.VMEM((32 * OWN, ROWS), F32),
                 pltpu.VMEM((4, 2, 64, 128), F32),
-                pltpu.VMEM((4, 64, 128), F32),
+                pltpu.VMEM((HOME + 1, 4, 64, 128), F32),
                 pltpu.VMEM((2, 64, 128), F32),
                 dma((6,)),
                 dma((2, 3)),
@@ -603,8 +663,8 @@
                 dma,
                 dma,
                 dma((slices,)),
-                dma((2, rounds)),
-                dma((2, rounds)),
+                dma((4, rounds)),
+                dma((4, rounds)),
                 dma((slices,)),
                 dma((slices,)),
                 dma,
@@ -613,11 +673,12 @@
                 dma,
                 dma((4,)),
                 dma((2,)),
-                dma((4,)),
+                dma((HOME + 1, 4)),
                 dma((2,)),
+                pltpu.SemaphoreType.REGULAR,
             ],
             compiler_params=pltpu.CompilerParams(
-                collective_id=0, has_side_effects=True, vmem_limit_bytes=36 * 2**20
+                collective_id=0, has_side_effects=True, vmem_limit_bytes=56 * 2**20
             ),
             cost_estimate=pl.CostEstimate(flops=flops, bytes_accessed=2**21, transcendentals=2**18),
         )(phase, tilt, intensity, *constants)

time: 113 us -> 105 us (0.929)
  Pallas kernels: 106 us -> 101 us
  local copies, waits for them, and re-layouts: 6.34 us -> 2.94 us
    pallas_call x1, Pallas kernels: 106 us -> 101 us  [body(): pl.pallas_call(functools.partial(kernel, depth, cols, y_lo, slices), out_...]
    unnamed x14 -> x2, local copies, waits for them, and re-layouts: 6.34 us -> 2.94 us
where the time goes in v6:
time: 105 us; the launch traced here: 104 us
  Pallas kernels  101 us (96%)
  local copies, waits for them, and re-layouts  2.94 us (3%)
    pallas_call x1, Pallas kernels, body(): pl.pallas_call(functools.partial(kernel, depth, cols, y_lo, slices), out_...  101 us
    unnamed x2, local copies, waits for them, and re-layouts  2.94 us

profile of v6, /device:TPU:57, one launch (start us, length us, event | category | flops | bytes accessed | tf_op | source)
XLA Modules:
  0.0 104.5 jit_solution(12254452524595918135)
XLA Ops:
  0.6 100.9 %shard_map.77 = (f32[1,64,128]{2,1,0:T(8,128)}, f32[2,1,2,64,128]{4,3,2,1,0:T(8,128)}) custom-call(f32[1,64,128]{2,1,0:T(8,128)} %phase_h.1, s32[2,2]{1,0:T(2,128)} %tilt_h.1, f32[2,64,128]{2,1,0:T(8,128)} %intensity_h.1, bf16[256,512]{1,0:T(8,128)(2,1)} %constant.6.clone.row_high_h, bf16[256,512]{1,0:T(8,128)(2,1)} %constant.7.clone.row_low_h, ...), custom_call_target="tpu_custom_call" | custom-call | flops 12683575296 | bytes 2097152 | tf_op jit(solution)/shard_map/pallas_call | solution.py:629
  101.6 1.4 %copy.10 = f32[1,64,128]{2,1,0:T(8,128)} copy(f32[1,64,128]{2,1,0:T(8,128)} %get-tuple-element.4) | data formatting | bytes 65536
  102.9 1.6 %copy.11 = f32[2,1,2,64,128]{4,3,2,1,0:T(8,128)} copy(f32[2,1,2,64,128]{4,3,2,1,0:T(8,128)} %get-tuple-element.5) | data formatting | bytes 262144

commit v7 on v6

--- a/solution.py
+++ b/solution.py
@@ -220,6 +220,32 @@
 
     loads[0].wait()
     loads[1].wait()
+    loads[2].wait()
+
+    @pl.when(worker)
+    def _():
+        @pl.when(strip == 0)
+        def _():
+            @pl.loop(0, 2 * rounds)
+            def _(k):
+                spread[k, pl.ds(0, side)] = jnp.zeros((side, ROWS), F32)
+
+        @pl.when(strip == cols - 1)
+        def _():
+            @pl.loop(0, 2 * rounds)
+            def _(k):
+                spread[k, pl.ds(side + own_rows, side)] = jnp.zeros((side, ROWS), F32)
+
+        row_pos = lax.broadcasted_iota(jnp.int32, (32 * OWN, ROWS), 1).astype(F32)
+        col_pos = (strip * (32 * OWN) + lax.broadcasted_iota(jnp.int32, (32 * OWN, ROWS), 0)).astype(F32)
+        t0, t1 = tilt[b, 0].astype(F32), tilt[b, 1].astype(F32)
+        angle = 2.0 * jnp.pi * (t0 * row_pos / float(ROWS) + t1 * col_pos / float(cols * 32 * OWN))
+        cos, sin = jnp.cos(angle), jnp.sin(angle)
+        incident = []
+        for g in range(OWN):
+            incident += [cos[32 * g : 32 * g + 32], sin[32 * g : 32 * g + 32]]
+        entering[0] = jnp.concatenate(incident, axis=0)
+
     pl.semaphore_wait(barrier, expected)
 
     def ready_signal(condition, device):
@@ -291,10 +317,13 @@
         def _():
             push(*own_args())
 
-    for load in loads[2:]:
+    for load in loads[3:]:
         load.wait()
 
     def row_step(value):
+        if value.shape[0] > 128:
+            cuts = range(0, value.shape[0], 128)
+            return jnp.concatenate([row_step(value[c : c + 128]) for c in cuts], axis=0)
         high, low = split(value)
         full = dot(high, row_high[...]) + (dot(low, row_high[...]) + dot(high, row_low[...]))
         out = []
@@ -443,20 +472,24 @@
         for i in range(2, RUN + 1):
             out = RUN - i
             j = first_slice + i - 1
+            if i == RUN and not last:
+                get_screen(j + 1, False)
+                for p in range(2):
+                    span = pl.ds(128 * p, 128)
+                    wave = col_step(work[pl.ds(128 * p, 256)])
+                    leaving[j, span] = wave
+                    after = cmul(screens[j + 1, pl.ds(64 * rim + 128 * p, 128)], wave)
+                    entering[j + 1, span] = after
+                    spread[k + 1, pl.ds(side + 128 * p, 128)] = row_step(after)
+                continue
             wave = col_step(next_input(i))
             leaving[j] = own_part(wave, out)
             if i < RUN:
                 leave_start(j)
-            elif not last:
-                get_screen(j + 1, False)
             if i < RUN:
                 after = cmul(screen_on(j + 1, out), wave)
                 entering[j + 1] = own_part(after, out)
                 work[pl.ds(0, 64 * (OWN + 2 * out))] = row_step(after)
-            elif not last:
-                after = cmul(screen_on(j + 1, 0), wave)
-                entering[j + 1] = after
-                spread[k + 1, pl.ds(side, own_rows)] = row_step(after)
             else:
                 arrived(levels_in, level_r)
                 level = jnp.concatenate([turn_tiles(levels_in, h) for h in range(2)], axis=1)
@@ -477,12 +510,21 @@
         for i in range(2, RUN + 1):
             out = RUN - i
             j = first_slice - (i - 1)
+            if i == RUN and not last:
+                for p in range(2):
+                    pulled = col_step(work[pl.ds(128 * p, 256)])
+                    onward = row_step(cmul(screens[j, pl.ds(64 * rim + 128 * p, 128)], pulled))
+                    spread[k + 1, pl.ds(side + 128 * p, 128)] = onward
+                    parts = []
+                    for (pr, pi), (er, ei) in zip(blocks_of(pulled), blocks_of(entering[j, pl.ds(128 * p, 128)])):
+                        parts.append(-(pr * ei + pi * er))
+                    grads[j, pl.ds(64 * p, 64)] = jnp.concatenate(parts, axis=0)
+                halo_start(k + 1)
+                grads_start(j)
+                continue
             pulled = col_step(next_input(i))
             if i < RUN:
                 work[pl.ds(0, 64 * (OWN + 2 * out))] = row_step(cmul(screen_on(j, out), pulled))
-            elif not last:
-                spread[k + 1, pl.ds(side, own_rows)] = row_step(cmul(screen_on(j, 0), pulled))
-                halo_start(k + 1)
             parts = []
             for (pr, pi), (er, ei) in zip(blocks_of(own_part(pulled, out)), blocks_of(entering[j])):
                 parts.append(-(pr * ei + pi * er))
@@ -497,28 +539,8 @@
 
     @pl.when(worker)
     def _():
-        @pl.when(strip == 0)
-        def _():
-            @pl.loop(0, 2 * rounds)
-            def _(k):
-                spread[k, pl.ds(0, side)] = jnp.zeros((side, ROWS), F32)
-
-        @pl.when(strip == cols - 1)
-        def _():
-            @pl.loop(0, 2 * rounds)
-            def _(k):
-                spread[k, pl.ds(side + own_rows, side)] = jnp.zeros((side, ROWS), F32)
-
-        row_pos = lax.broadcasted_iota(jnp.int32, (32 * OWN, ROWS), 1).astype(F32)
-        col_pos = (strip * (32 * OWN) + lax.broadcasted_iota(jnp.int32, (32 * OWN, ROWS), 0)).astype(F32)
-        t0, t1 = tilt[b, 0].astype(F32), tilt[b, 1].astype(F32)
-        angle = 2.0 * jnp.pi * (t0 * row_pos / float(ROWS) + t1 * col_pos / float(cols * 32 * OWN))
-        cos, sin = jnp.cos(angle), jnp.sin(angle)
-        incident = []
-        for g in range(OWN):
-            incident += [cos[32 * g : 32 * g + 32], sin[32 * g : 32 * g + 32]]
         get_screen(0, False)
-        start = cmul(screen_on(0, 0), jnp.concatenate(incident, axis=0))
+        start = cmul(screen_on(0, 0), entering[0])
         entering[0] = start
         spread[0, pl.ds(side, own_rows)] = row_step(start)
 

time: 105 us -> 99.4 us (0.947)
  Pallas kernels: 101 us -> 95.6 us
    pallas_call x1, Pallas kernels: 101 us -> 95.6 us  [body(): pl.pallas_call(functools.partial(kernel, depth, cols, y_lo, slices), out_...]
where the time goes in v7:
time: 99.4 us; the launch traced here: 99.2 us
  Pallas kernels  95.6 us (96%)
  local copies, waits for them, and re-layouts  2.94 us (3%)
    pallas_call x1, Pallas kernels, body(): pl.pallas_call(functools.partial(kernel, depth, cols, y_lo, slices), out_...  95.6 us
    unnamed x2, local copies, waits for them, and re-layouts  2.94 us

profile of v7, /device:TPU:57, one launch (start us, length us, event | category | flops | bytes accessed | tf_op | source)
XLA Modules:
  0.0 99.2 jit_solution(6886343687508028931)
XLA Ops:
  0.6 95.6 %shard_map.77 = (f32[1,64,128]{2,1,0:T(8,128)}, f32[2,1,2,64,128]{4,3,2,1,0:T(8,128)}) custom-call(f32[1,64,128]{2,1,0:T(8,128)} %phase_h.1, s32[2,2]{1,0:T(2,128)} %tilt_h.1, f32[2,64,128]{2,1,0:T(8,128)} %intensity_h.1, bf16[256,512]{1,0:T(8,128)(2,1)} %constant.6.clone.row_high_h, bf16[256,512]{1,0:T(8,128)(2,1)} %constant.7.clone.row_low_h, ...), custom_call_target="tpu_custom_call" | custom-call | flops 12683575296 | bytes 2097152 | tf_op jit(solution)/shard_map/pallas_call | solution.py:651
  96.2 1.4 %copy.10 = f32[1,64,128]{2,1,0:T(8,128)} copy(f32[1,64,128]{2,1,0:T(8,128)} %get-tuple-element.4) | data formatting | bytes 65536
  97.6 1.6 %copy.11 = f32[2,1,2,64,128]{4,3,2,1,0:T(8,128)} copy(f32[2,1,2,64,128]{4,3,2,1,0:T(8,128)} %get-tuple-element.5) | data formatting | bytes 262144

commit v8 on v7

--- a/solution.py
+++ b/solution.py
@@ -321,9 +321,9 @@
         load.wait()
 
     def row_step(value):
-        if value.shape[0] > 128:
-            cuts = range(0, value.shape[0], 128)
-            return jnp.concatenate([row_step(value[c : c + 128]) for c in cuts], axis=0)
+        if value.shape[0] > 64:
+            cuts = range(0, value.shape[0], 64)
+            return jnp.concatenate([row_step(value[c : c + 64]) for c in cuts], axis=0)
         high, low = split(value)
         full = dot(high, row_high[...]) + (dot(low, row_high[...]) + dot(high, row_low[...]))
         out = []

time: 99.4 us -> 106 us (1.066)
  Pallas kernels: 95.6 us -> 102 us
    pallas_call x1, Pallas kernels: 95.6 us -> 102 us  [body(): pl.pallas_call(functools.partial(kernel, depth, cols, y_lo, slices), out_...]
where the time goes in v8:
time: 106 us; the launch traced here: 105 us
  Pallas kernels  102 us (96%)
  local copies, waits for them, and re-layouts  2.94 us (3%)
    pallas_call x1, Pallas kernels, body(): pl.pallas_call(functools.partial(kernel, depth, cols, y_lo, slices), out_...  102 us
    unnamed x2, local copies, waits for them, and re-layouts  2.94 us

profile of v8, /device:TPU:57, one launch (start us, length us, event | category | flops | bytes accessed | tf_op | source)
XLA Modules:
  0.0 105.3 jit_solution(5687561466807792733)
XLA Ops:
  0.6 101.7 %shard_map.77 = (f32[1,64,128]{2,1,0:T(8,128)}, f32[2,1,2,64,128]{4,3,2,1,0:T(8,128)}) custom-call(f32[1,64,128]{2,1,0:T(8,128)} %phase_h.1, s32[2,2]{1,0:T(2,128)} %tilt_h.1, f32[2,64,128]{2,1,0:T(8,128)} %intensity_h.1, bf16[256,512]{1,0:T(8,128)(2,1)} %constant.6.clone.row_high_h, bf16[256,512]{1,0:T(8,128)(2,1)} %constant.7.clone.row_low_h, ...), custom_call_target="tpu_custom_call" | custom-call | flops 12683575296 | bytes 2097152 | tf_op jit(solution)/shard_map/pallas_call | solution.py:651
  102.4 1.4 %copy.10 = f32[1,64,128]{2,1,0:T(8,128)} copy(f32[1,64,128]{2,1,0:T(8,128)} %get-tuple-element.4) | data formatting | bytes 65536
  103.8 1.6 %copy.11 = f32[2,1,2,64,128]{4,3,2,1,0:T(8,128)} copy(f32[2,1,2,64,128]{4,3,2,1,0:T(8,128)} %get-tuple-element.5) | data formatting | bytes 262144
